TPU v7x, 32 devices: a whole 2x2x4 slice. The times are simulated.
32 devices in a mesh: grp: 2 (over x), blk: 16 (over z, y, core).
Axes of the slice: x: 2, y: 2, z: 4, core: 2. Of those that a mesh axis runs over, the one named last changes fastest.
Arguments:
- features: bfloat16 [512, 64, 256], P(('grp', 'blk')), parts along dimension 0, may hold values from -6 to 6
- occupancy: int32 [512, 64], P(('grp', 'blk')), parts along dimension 0, may hold values 0 or 1
- neighbors: int32 [512, 6], P(('grp', 'blk')), parts along dimension 0, may hold values from -1 to 15
- previous: bfloat16 [512, 64, 256], P(('grp', 'blk')), parts along dimension 0, may hold values from -6 to 6
- old_owner: int32 [512, 1], P(('grp', 'blk')), parts along dimension 0, may hold values from 0 to 15; in each aligned block of 16 rows (0 to 15, 16 to 31, ...) at most 2 rows name the same one
- old_slot: int32 [512], P(('grp', 'blk')), parts along dimension 0, may hold values from 0 to 15
- conv_weight: bfloat16 [27, 256, 256], replicated, may hold values from -0.078125 to 0.078125
- norm_scale: float32 [256], replicated, may hold values from 0.1 to 1.9
- norm_shift: float32 [256], replicated, may hold values from -3 to 3
- prev_weight: bfloat16 [256, 256], replicated, may hold values from -0.375 to 0.375
Outputs:
- merged: bfloat16 [512, 64, 256], P(('grp', 'blk')), parts along dimension 0
There are 2 independent parts, one for each index of `grp`. A program takes and returns all parts, laid end to end along the dimension named above; an argument that names none is the same for every part. Nothing has to cross between parts.
Inputs may be any that keep to these rules, and one draw needn't show every extreme that they name: `old_owner`: among the 16 block slots of one device, at most 2 name the same old owner.
All inputs are finite; a program needn't handle non-finite values. No bound on the sum of `occupancy` on one device may be relied on, other than what follows from the above.
Results may differ from a plain program's by a relative error of at most 0.0034.
Values may be sent and summed in bfloat16 or wider, within the bound.
No kernel may reach another device: no remote copies, remote signals or barrier semaphores. Data moves between devices by JAX's collectives and lax.ppermute only.
A program may use at most 128 MiB of HBM per device.

v0:
```python
import jax
import jax.numpy as jnp
from jax import lax
from jax.sharding import PartitionSpec as P

EDGE = 4


def with_halo(cells, sides, width):
    for axis, dim in sides:
        count = lax.axis_size(axis)
        ends = count - 1
        head = lax.slice_in_dim(cells, 0, width, axis=dim)
        tail = lax.slice_in_dim(cells, cells.shape[dim] - width, cells.shape[dim], axis=dim)
        cells = jnp.concatenate(
            [
                lax.ppermute(tail, axis, [(i, (i + 1) % count) for i in range(ends)]),
                cells,
                lax.ppermute(head, axis, [((i + 1) % count, i) for i in range(ends)]),
            ],
            axis=dim,
        )
    return cells


def pick_layers(source_layers, slots):
    valid = (slots >= 0).astype(jnp.bfloat16)
    chosen = jnp.take(source_layers, jnp.clip(slots, 0, source_layers.shape[0] - 1), axis=0)
    return chosen * valid[:, None, None, None]


def per_device(
    features,
    occupancy,
    neighbors,
    previous,
    old_owner,
    old_slot,
    conv_weight,
    norm_scale,
    norm_shift,
    prev_weight,
):
    slot_count = features.shape[0]
    channels = features.shape[2]
    peer_count = lax.axis_size("blk")
    cap = max(2, 2 * slot_count // peer_count)
    occ_mask = occupancy.astype(jnp.bfloat16)[:, :, None]
    masked = features * occ_mask
    cube = masked.reshape(slot_count, EDGE, EDGE, EDGE, channels)
    stacked = jnp.stack([cube[:, 0], cube[:, EDGE - 1]])
    rimmed = with_halo(stacked, (("blk", 0),), 1)
    from_lower = rimmed[0]
    from_upper = rimmed[3]
    volume = jnp.zeros((slot_count, EDGE + 2, EDGE + 2, EDGE + 2, channels), jnp.bfloat16)
    volume = volume.at[:, 1 : EDGE + 1, 1 : EDGE + 1, 1 : EDGE + 1].set(cube)
    volume = volume.at[:, 0, 1 : EDGE + 1, 1 : EDGE + 1].set(
        pick_layers(from_lower, neighbors[:, 0])
    )
    volume = volume.at[:, EDGE + 1, 1 : EDGE + 1, 1 : EDGE + 1].set(
        pick_layers(from_upper, neighbors[:, 1])
    )
    volume = volume.at[:, 1 : EDGE + 1, 0, 1 : EDGE + 1].set(
        pick_layers(cube[:, :, EDGE - 1], neighbors[:, 2])
    )
    volume = volume.at[:, 1 : EDGE + 1, EDGE + 1, 1 : EDGE + 1].set(
        pick_layers(cube[:, :, 0], neighbors[:, 3])
    )
    volume = volume.at[:, 1 : EDGE + 1, 1 : EDGE + 1, 0].set(
        pick_layers(cube[:, :, :, EDGE - 1], neighbors[:, 4])
    )
    volume = volume.at[:, 1 : EDGE + 1, 1 : EDGE + 1, EDGE + 1].set(
        pick_layers(cube[:, :, :, 0], neighbors[:, 5])
    )
    conv_out = jnp.zeros((slot_count * EDGE * EDGE * EDGE, channels), jnp.float32)
    for shift_a in range(3):
        for shift_b in range(3):
            windows = [
                volume[
                    :, shift_a : shift_a + EDGE, shift_b : shift_b + EDGE, shift_c : shift_c + EDGE
                ]
                for shift_c in range(3)
            ]
            joined = jnp.concatenate(windows, axis=-1).reshape(-1, 3 * channels)
            first_tap = (3 * shift_a + shift_b) * 3
            weight_rows = conv_weight[first_tap : first_tap + 3].reshape(3 * channels, channels)
            conv_out = conv_out + jnp.dot(joined, weight_rows, preferred_element_type=jnp.float32)
    hidden = jnp.maximum(conv_out * norm_scale[None, :] + norm_shift[None, :], 0.0)
    owners = old_owner[:, 0]
    slot_ids = jnp.arange(slot_count, dtype=jnp.int32)
    same_owner = owners[:, None] == owners[None, :]
    earlier = slot_ids[None, :] < slot_ids[:, None]
    order_rank = jnp.sum((same_owner & earlier).astype(jnp.int32), axis=1)
    position = owners * cap + order_rank
    buffer_ids = jnp.arange(peer_count * cap, dtype=jnp.int32)
    matches = position[None, :] == buffer_ids[:, None]
    wanted = jnp.sum(matches.astype(jnp.int32) * old_slot[None, :], axis=1)
    outgoing = jnp.where(jnp.any(matches, axis=1), wanted, -1)
    incoming = lax.all_to_all(outgoing, "blk", split_axis=0, concat_axis=0, tiled=True)
    present = (incoming >= 0).astype(jnp.bfloat16)
    replies = (
        jnp.take(previous, jnp.clip(incoming, 0, slot_count - 1), axis=0) * present[:, None, None]
    )
    returned = lax.all_to_all(replies, "blk", split_axis=0, concat_axis=0, tiled=True)
    picked = jnp.take(returned, position, axis=0)
    projected = jnp.dot(
        picked.reshape(-1, channels), prev_weight, preferred_element_type=jnp.float32
    ).astype(jnp.bfloat16)
    projected = lax.optimization_barrier(projected)
    occ_float = occupancy.astype(jnp.float32).reshape(-1, 1)
    merged = (hidden + projected.astype(jnp.float32)) * occ_float
    return merged.reshape(slot_count, EDGE * EDGE * EDGE, channels).astype(jnp.bfloat16)


def solution(mesh):
    in_specs = (
        P(("grp", "blk"), None, None),
        P(("grp", "blk"), None),
        P(("grp", "blk"), None),
        P(("grp", "blk"), None, None),
        P(("grp", "blk"), None),
        P(("grp", "blk")),
        P(),
        P(),
        P(),
        P(),
    )
    out_specs = P(("grp", "blk"), None, None)
    return jax.shard_map(
        per_device, mesh=mesh, in_specs=in_specs, out_specs=out_specs, check_vma=False
    )
```

profile of v0, /device:TPU:11, one launch (start us, length us, event | category | flops | bytes accessed | tf_op | source)
XLA Modules:
  0.0 105.1 jit_solution(16008034880931194272)
XLA Ops:
  0.0 0.8 fusion.26
  0.9 1.4 %copy_multiply_fusion = bf16[16,64,256]{2,0,1:T(8,128)(2,1)S(1)} fusion(bf16[16,64,256]{2,1,0:T(8,128)(2,1)} %param.26, bf16[16,64]{0,1:T(8,128)(2,1)S(1)} %copy.87), kind=kLoop, calls=%fused_computation.34 | loop fusion | flops 262144 | bytes 1050624 | tf_op jit(solution)/shard_map/mul | solution.py:49
  2.3 0.7 copy.129
  3.0 3.7 %collective-permute-start = (bf16[1,16,4,4,256]{4,3,2,1,0:T(4,128)(2,1)}, bf16[1,16,4,4,256]{4,3,2,1,0:T(4,128)(2,1)}, u32[]{:S(2)}, u32[]{:S(2)}) collective-permute-start(bf16[1,16,4,4,256]{4,3,2,1,0:T(4,128)(2,1)} %bitcast.106), channel_id=1, source_target_pairs={{0,1},{1,2},{2,3},{3,4},{4,5},{5,6},{6,7},{7,8},{8,9},{9,10},{10,1... | collective-permute-start | bytes 393224 | tf_op jit(solution)/shard_map/ppermute | solution.py:17
  6.7 0.7 copy.128
  7.4 1.9 %collective-permute-start.1 = (bf16[1,16,4,4,256]{4,3,2,1,0:T(4,128)(2,1)}, bf16[1,16,4,4,256]{4,3,2,1,0:T(4,128)(2,1)}, u32[]{:S(2)}, u32[]{:S(2)}) collective-permute-start(bf16[1,16,4,4,256]{4,3,2,1,0:T(4,128)(2,1)} %bitcast.105), channel_id=1, source_target_pairs={{1,0},{2,1},{3,2},{4,3},{5,4},{6,5},{7,6},{8,7},{9,8},{10,9},{11,1... | collective-permute-start | bytes 393224 | tf_op jit(solution)/shard_map/ppermute | solution.py:19
  9.8 0.7 select_n.54
  10.4 6.5 %all-to-all-start = ((s32[16,2,1]{1,2,0:T(1,128)}), s32[16,2,1]{1,2,0:T(1,128)S(1)}, u32[]{:S(2)}, u32[]{:S(2)}) async-start(s32[16,2,1]{1,2,0:T(1,128)} %bitcast.39), calls=%async_computation | async-start | bytes 16384 | tf_op jit(solution)/shard_map/all_to_all | solution.py:99
  17.7 1.4 %copy-done.13 = bf16[27,256,256]{2,1,0:T(8,128)(2,1)S(1)} copy-done((bf16[27,256,256]{2,1,0:T(8,128)(2,1)S(1)}, bf16[27,256,256]{2,1,0:T(8,128)(2,1)}, u32[]{:S(2)}) %copy-start.13) | copy-done | bytes 3538968
  19.1 1.8 %fusion.21 = (bf16[3,256,256]{2,1,0:T(8,128)(2,1)}, bf16[3,256,256]{2,1,0:T(8,128)(2,1)}, bf16[3,256,256]{2,1,0:T(8,128)(2,1)}, bf16[3,256,256]{2,1,0:T(8,128)(2...) fusion(bf16[27,256,256]{2,1,0:T(8,128)(2,1)S(1)} %copy-done.13), kind=kLoop, calls=%fused_computation.108 | loop fusion | bytes 7077888 | tf_op jit(solution)/shard_map/slice | solution.py:86
  20.9 0.7 gather_fusion.5
  21.5 0.7 gather_fusion.4
  22.2 0.7 gather_fusion.7
  22.9 0.7 gather_fusion.6
  23.5 0.9 fusion.6
  24.4 1.0 select_multiply_fusion.1
  26.0 0.6 gather_fusion
  26.6 1.1 %select_multiply_fusion = bf16[32,64,256]{2,1,0:T(8,128)(2,1)} fusion(bf16[32,64,256]{2,1,0:T(8,128)(2,1)S(1)} %gather_fusion, pred[32]{0:T(512)(128)(4,1)S(1)} %compare_and_fusion.6, bf16[32]{0:T(256)(128)(2,1)S(1)} %reshape.577), kind=kLoop, calls=%fused_computation.32 | loop fusion | flops 1048576 | bytes 2097248 | tf_op jit(solution)/shard_map/mul | solution.py:102
  27.8 6.1 %all-to-all-start.1 = ((bf16[32,64,256]{2,1,0:T(8,128)(2,1)}), bf16[32,64,256]{2,1,0:T(8,128)(2,1)}, u32[]{:S(2)}, u32[]{:S(2)}) async-start(bf16[32,64,256]{2,1,0:T(8,128)(2,1)} %select_multiply_fusion), calls=%async_computation.1 | async-start | bytes 2097152 | tf_op jit(solution)/shard_map/all_to_all | solution.py:104
  34.0 1.6 %gather_fusion.2 = bf16[16,4,4,256]{3,2,1,0:T(4,128)(2,1)S(1)} fusion(bf16[16,4,4,256]{3,2,1,0:T(4,128)(2,1)} %bitcast.3, s32[1024]{0:T(1024)S(1)} %pad_clamp_fusion.7), kind=kCustom, calls=%fused_computation.clone | custom fusion | bytes 262208 | tf_op jit(solution)/shard_map/jit(_take)/gather | solution.py:28
  35.8 1.6 %gather_fusion.3 = bf16[16,4,4,256]{3,2,1,0:T(4,128)(2,1)S(1)} fusion(bf16[16,4,4,256]{3,2,1,0:T(4,128)(2,1)} %bitcast.8, s32[1024]{0:T(1024)S(1)} %pad_clamp_fusion.6), kind=kCustom, calls=%fused_computation.1.clone | custom fusion | bytes 262208 | tf_op jit(solution)/shard_map/jit(_take)/gather | solution.py:28
  37.8 1.5 %fusion.23 = (bf16[16,4,4,4,256]{4,0,3,2,1:T(8,128)(2,1)}, bf16[16,4,4,4,256]{4,0,3,2,1:T(8,128)(2,1)}, bf16[16,4,4,4,256]{4,0,3,2,1:T(8,128)(2,1)}, bf16[16,4,4...) fusion(bf16[16,6,6,6,256]{4,0,3,2,1:T(8,128)(2,1)S(1)} %bitcast, ...), kind=kLoop, calls=%fused_computation.110 | loop fusion | bytes 8388608 | tf_op jit(solution)/shard_map/slice | solution.py:79
  39.3 3.9 %fusion.22 = (bf16[16,4,4,4,256]{4,0,3,2,1:T(8,128)(2,1)}, bf16[16,4,4,4,256]{4,0,3,2,1:T(8,128)(2,1)}, bf16[16,4,4,4,256]{4,0,3,2,1:T(8,128)(2,1)}, bf16[16,4,4...) fusion(bf16[16,6,6,6,256]{4,0,3,2,1:T(8,128)(2,1)S(1)} %bitcast, ...), kind=kLoop, calls=%fused_computation.109 | loop fusion | bytes 19922944 | tf_op jit(solution)/shard_map/slice | solution.py:79
  43.4 0.8 copy.101
  44.6 1.5 %pad_maximum_fusion.1 = bf16[16,4,4,4,768]{4,0,3,2,1:T(8,128)(2,1)S(1)} fusion(bf16[16,4,4,4,256]{4,0,3,2,1:T(8,128)(2,1)} %get-tuple-element.134, bf16[16,4,4,4,256]{4,0,3,2,1:T(8,128)(2,1)} %get-tuple-element.135, bf16[16,4,4,4,256]{4,0,3,2,1:T(8,128)(2,1)} %get-tuple-element.136), kind=kLoop, calls=%fused_computation.9 | loop fusion | flops 4718592 | bytes 3145728 | tf_op jit(solution)/shard_map/concatenate | solution.py:84
  46.1 0.8 copy.102
  46.9 1.4 %reshape.555 = bf16[1024,768]{1,0:T(8,128)(2,1)} reshape(bf16[16,4,4,4,768]{4,3,2,1,0:T(4,128)(2,1)S(1)} %copy.102) | data formatting | bytes 3145728 | tf_op jit(solution)/shard_map/reshape | solution.py:84
  48.3 0.6 fusion.27
  48.9 0.8 copy-done.12
  49.8 1.6 %convolution_add_fusion.7 = f32[1024,256]{1,0:T(8,128)} fusion(f32[1024,256]{1,0:T(8,128)S(1)} %fusion.27, bf16[1024,768]{1,0:T(8,128)(2,1)S(1)} %copy-done.12, bf16[768,256]{1,0:T(8,128)(2,1)S(1)} %bitcast.118), kind=kOutput, calls=%fused_computation.29 | convolution fusion | flops 402915328 | bytes 4063232 | tf_op jit(solution)/shard_map/dot_general | solution.py:87
  51.5 0.9 copy-done.29
  52.9 0.9 copy-done.26
  54.2 0.9 copy-done.23
  55.4 1.3 %pad_maximum_fusion.5 = bf16[16,4,4,4,768]{4,0,3,2,1:T(8,128)(2,1)} fusion(bf16[16,4,4,4,256]{4,0,3,2,1:T(8,128)(2,1)S(1)} %copy-done.23, bf16[16,4,4,4,256]{4,0,3,2,1:T(8,128)(2,1)S(1)} %copy-done.24, bf16[16,4,4,4,256]{4,0,3,2,1:T(8,128)(2,1)S(1)} %copy-done.25), kind=kLoop, calls=%fused_computation.13 | loop fusion | flops 4718592 | bytes 3145728 | tf_op jit(solution)/shard_map/concatenate | solution.py:84
  57.4 1.3 %pad_maximum_fusion.6 = bf16[16,4,4,4,768]{4,0,3,2,1:T(8,128)(2,1)} fusion(bf16[16,4,4,4,256]{4,0,3,2,1:T(8,128)(2,1)S(1)} %copy-done.20, bf16[16,4,4,4,256]{4,0,3,2,1:T(8,128)(2,1)S(1)} %copy-done.21, bf16[16,4,4,4,256]{4,0,3,2,1:T(8,128)(2,1)S(1)} %copy-done.22), kind=kLoop, calls=%fused_computation.14 | loop fusion | flops 4718592 | bytes 3145728 | tf_op jit(solution)/shard_map/concatenate | solution.py:84
  59.3 1.3 %pad_maximum_fusion.7 = bf16[16,4,4,4,768]{4,0,3,2,1:T(8,128)(2,1)} fusion(bf16[16,4,4,4,256]{4,0,3,2,1:T(8,128)(2,1)S(1)} %copy-done.17, bf16[16,4,4,4,256]{4,0,3,2,1:T(8,128)(2,1)S(1)} %copy-done.18, bf16[16,4,4,4,256]{4,0,3,2,1:T(8,128)(2,1)S(1)} %copy-done.19), kind=kLoop, calls=%fused_computation.15 | loop fusion | flops 4718592 | bytes 3145728 | tf_op jit(solution)/shard_map/concatenate | solution.py:84
  61.2 1.3 %pad_maximum_fusion.8 = bf16[16,4,4,4,768]{4,0,3,2,1:T(8,128)(2,1)} fusion(bf16[16,4,4,4,256]{4,0,3,2,1:T(8,128)(2,1)S(1)} %copy-done.15, bf16[16,4,4,4,256]{4,0,3,2,1:T(8,128)(2,1)S(1)} %copy-done.16, bf16[16,4,4,4,256]{4,0,3,2,1:T(8,128)(2,1)S(1)} %copy-done.14), kind=kLoop, calls=%fused_computation.16 | loop fusion | flops 4718592 | bytes 3145728 | tf_op jit(solution)/shard_map/concatenate | solution.py:84
  62.5 2.0 %copy.103 = bf16[16,4,4,4,768]{4,3,2,1,0:T(4,128)(2,1)} copy(bf16[16,4,4,4,768]{4,0,3,2,1:T(8,128)(2,1)S(1)} %pad_maximum_fusion.2) | data formatting | bytes 3145728 | tf_op jit(solution)/shard_map/concatenate | solution.py:84
  64.6 3.7 %reshape.557 = bf16[1024,768]{1,0:T(8,128)(2,1)} reshape(bf16[16,4,4,4,768]{4,3,2,1,0:T(4,128)(2,1)} %copy.103) | data formatting | bytes 3145728 | tf_op jit(solution)/shard_map/reshape | solution.py:84
  68.3 2.0 %copy.104 = bf16[16,4,4,4,768]{4,3,2,1,0:T(4,128)(2,1)} copy(bf16[16,4,4,4,768]{4,0,3,2,1:T(8,128)(2,1)S(1)} %pad_maximum_fusion.3) | data formatting | bytes 3145728 | tf_op jit(solution)/shard_map/concatenate | solution.py:84
  70.2 3.8 %reshape.559 = bf16[1024,768]{1,0:T(8,128)(2,1)} reshape(bf16[16,4,4,4,768]{4,3,2,1,0:T(4,128)(2,1)} %copy.104) | data formatting | bytes 3145728 | tf_op jit(solution)/shard_map/reshape | solution.py:84
  74.0 2.1 %copy.105 = bf16[16,4,4,4,768]{4,3,2,1,0:T(4,128)(2,1)} copy(bf16[16,4,4,4,768]{4,0,3,2,1:T(8,128)(2,1)S(1)} %pad_maximum_fusion.4) | data formatting | bytes 3145728 | tf_op jit(solution)/shard_map/concatenate | solution.py:84
  76.1 3.8 %reshape.561 = bf16[1024,768]{1,0:T(8,128)(2,1)} reshape(bf16[16,4,4,4,768]{4,3,2,1,0:T(4,128)(2,1)} %copy.105) | data formatting | bytes 3145728 | tf_op jit(solution)/shard_map/reshape | solution.py:84
  79.9 0.8 copy.106
  80.7 1.4 %reshape.563 = bf16[1024,768]{1,0:T(8,128)(2,1)} reshape(bf16[16,4,4,4,768]{4,3,2,1,0:T(4,128)(2,1)S(1)} %copy.106) | data formatting | bytes 3145728 | tf_op jit(solution)/shard_map/reshape | solution.py:84
  82.7 0.8 copy.107
  83.5 1.3 %reshape.565 = bf16[1024,768]{1,0:T(8,128)(2,1)} reshape(bf16[16,4,4,4,768]{4,3,2,1,0:T(4,128)(2,1)S(1)} %copy.107) | data formatting | bytes 3145728 | tf_op jit(solution)/shard_map/reshape | solution.py:84
  84.9 0.6 copy-done.4
  85.5 0.8 copy.108
  86.3 1.4 %reshape.567 = bf16[1024,768]{1,0:T(8,128)(2,1)} reshape(bf16[16,4,4,4,768]{4,3,2,1,0:T(4,128)(2,1)S(1)} %copy.108) | data formatting | bytes 3145728 | tf_op jit(solution)/shard_map/reshape | solution.py:84
  87.7 0.6 copy-done.5
  88.3 0.8 copy.109
  89.1 1.4 %reshape.569 = bf16[1024,768]{1,0:T(8,128)(2,1)} reshape(bf16[16,4,4,4,768]{4,3,2,1,0:T(4,128)(2,1)S(1)} %copy.109) | data formatting | bytes 3145728 | tf_op jit(solution)/shard_map/reshape | solution.py:84
  91.1 1.9 %convolution_add_fusion.6 = f32[1024,256]{1,0:T(8,128)S(1)} fusion(f32[1024,256]{1,0:T(8,128)} %convolution_add_fusion.7, bf16[1024,768]{1,0:T(8,128)(2,1)S(1)} %copy-done.6, bf16[768,256]{1,0:T(8,128)(2,1)S(1)} %bitcast.117), kind=kOutput, calls=%fused_computation.28 | convolution fusion | flops 402915328 | bytes 4063232 | tf_op jit(solution)/shard_map/dot_general | solution.py:87
  93.1 0.6 convolution_add_fusion.5
  93.7 0.8 copy-done.8
  95.1 0.8 copy-done.9
  96.0 0.6 convolution_add_fusion.3
  96.6 0.8 copy-done.10
  98.1 0.8 copy-done.11
  99.0 0.6 convolution_add_fusion.1
  99.6 1.9 %gather_fusion.1 = bf16[16,64,256]{2,1,0:T(8,128)(2,1)S(1)} fusion(bf16[32,64,256]{2,1,0:T(8,128)(2,1)} %all-to-all-done.1, s32[1024]{0:T(1024)S(1)} %pad_clamp_fusion), kind=kCustom, calls=%fused_computation.7 | custom fusion | bytes 1048640 | tf_op jit(solution)/shard_map/jit(_take)/gather | solution.py:105
  101.8 1.2 %convolution_convert_fusion = bf16[1024,256]{1,0:T(8,128)(2,1)S(1)} fusion(bf16[1024,256]{1,0:T(8,128)(2,1)S(1)} %bitcast_select_fusion, bf16[256,256]{1,0:T(8,128)(2,1)} %param.35), kind=kOutput, calls=%fused_computation.30 | convolution fusion | flops 134479872 | bytes 1179648 | tf_op jit(solution)/shard_map/dot_general | solution.py:106
  103.0 2.1 %fusion.5 = bf16[1024,256]{1,0:T(8,128)(2,1)} fusion(f32[1024,256]{1,0:T(8,128)S(1)} %convolution_add_fusion.1, bf16[1024,768]{1,0:T(8,128)(2,1)S(1)} %copy-done.35, bf16[768,256]{1,0:T(8,128)(2,1)S(1)} %bitcast.121, bf16[1024,256]{1,0:T(8,128)(2,1)S(1)} %convolution_convert_fusion, f32[1024]{0:T(1024)S(1)} %mul.123, f32[256]{0:T(256)S(1)} %copy-done.50, ...), kind=kOutput, calls=%fused_computation.31 | convolution fusion | flops 404750336 | bytes 4069376 | tf_op jit(solution)/shard_map/dot_general | solution.py:87
  (148 shorter events, 8.9 us)
Async XLA Ops:
  0.0 26.0 %copy-start = (bf16[16,64,256]{2,1,0:T(8,128)(2,1)S(1)}, bf16[16,64,256]{2,1,0:T(8,128)(2,1)}, u32[]{:S(2)}) copy-start(bf16[16,64,256]{2,1,0:T(8,128)(2,1)} %param.29) | copy-start | bytes 1572868
  0.0 9.4 %copy-start.49 = (s32[16,1]{0,1:T(1,128)S(1)}, s32[16,1]{0,1:T(1,128)}, u32[]{:S(2)}) copy-start(s32[16,1]{0,1:T(1,128)} %param.30) | copy-start | bytes 196
  0.0 9.7 %copy-start.51 = (s32[16]{0:T(128)S(1)}, s32[16]{0:T(128)}, u32[]{:S(2)}) copy-start(s32[16]{0:T(128)} %param.31) | copy-start | bytes 196
  0.0 17.0 %copy-start.48 = (s32[16,6]{0,1:T(8,128)S(1)}, s32[16,6]{0,1:T(8,128)}, u32[]{:S(2)}) copy-start(s32[16,6]{0,1:T(8,128)} %param.28) | copy-start | bytes 1156
  3.0 30.9 %collective-permute-start = (bf16[1,16,4,4,256]{4,3,2,1,0:T(4,128)(2,1)}, bf16[1,16,4,4,256]{4,3,2,1,0:T(4,128)(2,1)}, u32[]{:S(2)}, u32[]{:S(2)}) collective-permute-start(bf16[1,16,4,4,256]{4,3,2,1,0:T(4,128)(2,1)} %bitcast.106), channel_id=1, source_target_pairs={{0,1},{1,2},{2,3},{3,4},{4,5},{5,6},{6,7},{7,8},{8,9},{9,10},{10,1... | collective-permute-start | bytes 393224 | tf_op jit(solution)/shard_map/ppermute | solution.py:17
  7.4 28.3 %collective-permute-start.1 = (bf16[1,16,4,4,256]{4,3,2,1,0:T(4,128)(2,1)}, bf16[1,16,4,4,256]{4,3,2,1,0:T(4,128)(2,1)}, u32[]{:S(2)}, u32[]{:S(2)}) collective-permute-start(bf16[1,16,4,4,256]{4,3,2,1,0:T(4,128)(2,1)} %bitcast.105), channel_id=1, source_target_pairs={{1,0},{2,1},{3,2},{4,3},{5,4},{6,5},{7,6},{8,7},{9,8},{10,9},{11,1... | collective-permute-start | bytes 393224 | tf_op jit(solution)/shard_map/ppermute | solution.py:19
  10.4 15.2 %all-to-all-start = ((s32[16,2,1]{1,2,0:T(1,128)}), s32[16,2,1]{1,2,0:T(1,128)S(1)}, u32[]{:S(2)}, u32[]{:S(2)}) async-start(s32[16,2,1]{1,2,0:T(1,128)} %bitcast.39), calls=%async_computation | async-start | bytes 16384 | tf_op jit(solution)/shard_map/all_to_all | solution.py:99
  17.1 2.0 %copy-start.13 = (bf16[27,256,256]{2,1,0:T(8,128)(2,1)S(1)}, bf16[27,256,256]{2,1,0:T(8,128)(2,1)}, u32[]{:S(2)}) copy-start(bf16[27,256,256]{2,1,0:T(8,128)(2,1)} %param.32) | copy-start | bytes 10616836
  27.8 9.8 %copy-start.44 = (bf16[16,4,1,4,256]{4,3,1,0,2:T(4,128)(2,1)S(1)}, bf16[16,4,1,4,256]{4,3,1,0,2:T(4,128)(2,1)}, u32[]{:S(2)}) copy-start(bf16[16,4,1,4,256]{4,3,1,0,2:T(4,128)(2,1)} %get-tuple-element.169) | copy-start | bytes 393220
  27.8 71.8 %all-to-all-start.1 = ((bf16[32,64,256]{2,1,0:T(8,128)(2,1)}), bf16[32,64,256]{2,1,0:T(8,128)(2,1)}, u32[]{:S(2)}, u32[]{:S(2)}) async-start(bf16[32,64,256]{2,1,0:T(8,128)(2,1)} %select_multiply_fusion), calls=%async_computation.1 | async-start | bytes 2097152 | tf_op jit(solution)/shard_map/all_to_all | solution.py:104
  33.9 3.7 %copy-start.46 = (bf16[16,4,4,256]{3,2,1,0:T(4,128)(2,1)S(1)}, bf16[16,4,4,256]{3,2,1,0:T(4,128)(2,1)}, u32[]{:S(2)}) copy-start(bf16[16,4,4,256]{3,2,1,0:T(4,128)(2,1)} %get-tuple-element.167) | copy-start | bytes 393220
  33.9 3.8 %copy-start.45 = (bf16[16,4,4,256]{3,2,1,0:T(4,128)(2,1)S(1)}, bf16[16,4,4,256]{3,2,1,0:T(4,128)(2,1)}, u32[]{:S(2)}) copy-start(bf16[16,4,4,256]{3,2,1,0:T(4,128)(2,1)} %get-tuple-element.166) | copy-start | bytes 393220
  46.9 1.4 %copy-start.36 = (bf16[3,256,256]{2,1,0:T(8,128)(2,1)S(1)}, bf16[3,256,256]{2,1,0:T(8,128)(2,1)}, u32[]{:S(2)}) copy-start(bf16[3,256,256]{2,1,0:T(8,128)(2,1)} %get-tuple-element.111) | copy-start | bytes 1179652
  48.3 1.4 %copy-start.12 = (bf16[1024,768]{1,0:T(8,128)(2,1)S(1)}, bf16[1024,768]{1,0:T(8,128)(2,1)}, u32[]{:S(2)}) copy-start(bf16[1024,768]{1,0:T(8,128)(2,1)} %reshape.555) | copy-start | bytes 4718596
  48.3 1.5 %copy-start.43 = (bf16[3,256,256]{2,1,0:T(8,128)(2,1)S(1)}, bf16[3,256,256]{2,1,0:T(8,128)(2,1)}, u32[]{:S(2)}) copy-start(bf16[3,256,256]{2,1,0:T(8,128)(2,1)} %get-tuple-element.110) | copy-start | bytes 1179652
  49.8 1.6 %copy-start.32 = (bf16[16,4,4,4,256]{4,0,3,2,1:T(8,128)(2,1)S(1)}, bf16[16,4,4,4,256]{4,0,3,2,1:T(8,128)(2,1)}, u32[]{:S(2)}) copy-start(bf16[16,4,4,4,256]{4,0,3,2,1:T(8,128)(2,1)} %get-tuple-element.132) | copy-start | bytes 1572868
  49.8 1.6 %copy-start.33 = (bf16[16,4,4,4,256]{4,0,3,2,1:T(8,128)(2,1)S(1)}, bf16[16,4,4,4,256]{4,0,3,2,1:T(8,128)(2,1)}, u32[]{:S(2)}) copy-start(bf16[16,4,4,4,256]{4,0,3,2,1:T(8,128)(2,1)} %get-tuple-element.133) | copy-start | bytes 1572868
  49.8 1.6 %copy-start.34 = (bf16[16,4,4,4,256]{4,0,3,2,1:T(8,128)(2,1)S(1)}, bf16[16,4,4,4,256]{4,0,3,2,1:T(8,128)(2,1)}, u32[]{:S(2)}) copy-start(bf16[16,4,4,4,256]{4,0,3,2,1:T(8,128)(2,1)} %get-tuple-element.131) | copy-start | bytes 1572868
  51.4 1.0 copy-start.29
  51.4 1.2 %copy-start.30 = (bf16[16,4,4,4,256]{4,0,3,2,1:T(8,128)(2,1)S(1)}, bf16[16,4,4,4,256]{4,0,3,2,1:T(8,128)(2,1)}, u32[]{:S(2)}) copy-start(bf16[16,4,4,4,256]{4,0,3,2,1:T(8,128)(2,1)} %get-tuple-element.129) | copy-start | bytes 1572868
  51.4 1.3 %copy-start.31 = (bf16[16,4,4,4,256]{4,0,3,2,1:T(8,128)(2,1)S(1)}, bf16[16,4,4,4,256]{4,0,3,2,1:T(8,128)(2,1)}, u32[]{:S(2)}) copy-start(bf16[16,4,4,4,256]{4,0,3,2,1:T(8,128)(2,1)} %get-tuple-element.130) | copy-start | bytes 1572868
  52.7 1.0 copy-start.26
  52.7 1.2 %copy-start.27 = (bf16[16,4,4,4,256]{4,0,3,2,1:T(8,128)(2,1)S(1)}, bf16[16,4,4,4,256]{4,0,3,2,1:T(8,128)(2,1)}, u32[]{:S(2)}) copy-start(bf16[16,4,4,4,256]{4,0,3,2,1:T(8,128)(2,1)} %get-tuple-element.126) | copy-start | bytes 1572868
  52.7 1.4 %copy-start.28 = (bf16[16,4,4,4,256]{4,0,3,2,1:T(8,128)(2,1)S(1)}, bf16[16,4,4,4,256]{4,0,3,2,1:T(8,128)(2,1)}, u32[]{:S(2)}) copy-start(bf16[16,4,4,4,256]{4,0,3,2,1:T(8,128)(2,1)} %get-tuple-element.127) | copy-start | bytes 1572868
  54.1 1.0 copy-start.23
  54.1 1.2 %copy-start.24 = (bf16[16,4,4,4,256]{4,0,3,2,1:T(8,128)(2,1)S(1)}, bf16[16,4,4,4,256]{4,0,3,2,1:T(8,128)(2,1)}, u32[]{:S(2)}) copy-start(bf16[16,4,4,4,256]{4,0,3,2,1:T(8,128)(2,1)} %get-tuple-element.123) | copy-start | bytes 1572868
  54.1 1.4 %copy-start.25 = (bf16[16,4,4,4,256]{4,0,3,2,1:T(8,128)(2,1)S(1)}, bf16[16,4,4,4,256]{4,0,3,2,1:T(8,128)(2,1)}, u32[]{:S(2)}) copy-start(bf16[16,4,4,4,256]{4,0,3,2,1:T(8,128)(2,1)} %get-tuple-element.124) | copy-start | bytes 1572868
  55.4 1.3 %copy-start.20 = (bf16[16,4,4,4,256]{4,0,3,2,1:T(8,128)(2,1)S(1)}, bf16[16,4,4,4,256]{4,0,3,2,1:T(8,128)(2,1)}, u32[]{:S(2)}) copy-start(bf16[16,4,4,4,256]{4,0,3,2,1:T(8,128)(2,1)} %get-tuple-element.119) | copy-start | bytes 1572868
  55.4 1.6 %copy-start.21 = (bf16[16,4,4,4,256]{4,0,3,2,1:T(8,128)(2,1)S(1)}, bf16[16,4,4,4,256]{4,0,3,2,1:T(8,128)(2,1)}, u32[]{:S(2)}) copy-start(bf16[16,4,4,4,256]{4,0,3,2,1:T(8,128)(2,1)} %get-tuple-element.120) | copy-start | bytes 1572868
  55.4 1.9 %copy-start.22 = (bf16[16,4,4,4,256]{4,0,3,2,1:T(8,128)(2,1)S(1)}, bf16[16,4,4,4,256]{4,0,3,2,1:T(8,128)(2,1)}, u32[]{:S(2)}) copy-start(bf16[16,4,4,4,256]{4,0,3,2,1:T(8,128)(2,1)} %get-tuple-element.121) | copy-start | bytes 1572868
  57.4 1.3 %copy-start.17 = (bf16[16,4,4,4,256]{4,0,3,2,1:T(8,128)(2,1)S(1)}, bf16[16,4,4,4,256]{4,0,3,2,1:T(8,128)(2,1)}, u32[]{:S(2)}) copy-start(bf16[16,4,4,4,256]{4,0,3,2,1:T(8,128)(2,1)} %get-tuple-element.116) | copy-start | bytes 1572868
  57.4 1.6 %copy-start.18 = (bf16[16,4,4,4,256]{4,0,3,2,1:T(8,128)(2,1)S(1)}, bf16[16,4,4,4,256]{4,0,3,2,1:T(8,128)(2,1)}, u32[]{:S(2)}) copy-start(bf16[16,4,4,4,256]{4,0,3,2,1:T(8,128)(2,1)} %get-tuple-element.117) | copy-start | bytes 1572868
  57.4 1.9 %copy-start.19 = (bf16[16,4,4,4,256]{4,0,3,2,1:T(8,128)(2,1)S(1)}, bf16[16,4,4,4,256]{4,0,3,2,1:T(8,128)(2,1)}, u32[]{:S(2)}) copy-start(bf16[16,4,4,4,256]{4,0,3,2,1:T(8,128)(2,1)} %get-tuple-element.118) | copy-start | bytes 1572868
  59.3 1.3 %copy-start.14 = (bf16[16,4,4,4,256]{4,0,3,2,1:T(8,128)(2,1)S(1)}, bf16[16,4,4,4,256]{4,0,3,2,1:T(8,128)(2,1)}, u32[]{:S(2)}) copy-start(bf16[16,4,4,4,256]{4,0,3,2,1:T(8,128)(2,1)} %get-tuple-element.113) | copy-start | bytes 1572868
  59.3 1.6 %copy-start.15 = (bf16[16,4,4,4,256]{4,0,3,2,1:T(8,128)(2,1)S(1)}, bf16[16,4,4,4,256]{4,0,3,2,1:T(8,128)(2,1)}, u32[]{:S(2)}) copy-start(bf16[16,4,4,4,256]{4,0,3,2,1:T(8,128)(2,1)} %get-tuple-element.114) | copy-start | bytes 1572868
  59.3 1.9 %copy-start.16 = (bf16[16,4,4,4,256]{4,0,3,2,1:T(8,128)(2,1)S(1)}, bf16[16,4,4,4,256]{4,0,3,2,1:T(8,128)(2,1)}, u32[]{:S(2)}) copy-start(bf16[16,4,4,4,256]{4,0,3,2,1:T(8,128)(2,1)} %get-tuple-element.115) | copy-start | bytes 1572868
  76.1 3.8 %copy-start.2 = (bf16[16,4,4,4,768]{4,0,3,2,1:T(8,128)(2,1)S(1)}, bf16[16,4,4,4,768]{4,0,3,2,1:T(8,128)(2,1)}, u32[]{:S(2)}) copy-start(bf16[16,4,4,4,768]{4,0,3,2,1:T(8,128)(2,1)} %pad_maximum_fusion.5) | copy-start | bytes 4718596
  80.7 2.0 %copy-start.3 = (bf16[16,4,4,4,768]{4,0,3,2,1:T(8,128)(2,1)S(1)}, bf16[16,4,4,4,768]{4,0,3,2,1:T(8,128)(2,1)}, u32[]{:S(2)}) copy-start(bf16[16,4,4,4,768]{4,0,3,2,1:T(8,128)(2,1)} %pad_maximum_fusion.6) | copy-start | bytes 4718596
  83.5 2.0 %copy-start.4 = (bf16[16,4,4,4,768]{4,0,3,2,1:T(8,128)(2,1)S(1)}, bf16[16,4,4,4,768]{4,0,3,2,1:T(8,128)(2,1)}, u32[]{:S(2)}) copy-start(bf16[16,4,4,4,768]{4,0,3,2,1:T(8,128)(2,1)} %pad_maximum_fusion.7) | copy-start | bytes 4718596
  86.3 2.0 %copy-start.5 = (bf16[16,4,4,4,768]{4,0,3,2,1:T(8,128)(2,1)S(1)}, bf16[16,4,4,4,768]{4,0,3,2,1:T(8,128)(2,1)}, u32[]{:S(2)}) copy-start(bf16[16,4,4,4,768]{4,0,3,2,1:T(8,128)(2,1)} %pad_maximum_fusion.8) | copy-start | bytes 4718596
  89.1 2.0 %copy-start.6 = (bf16[1024,768]{1,0:T(8,128)(2,1)S(1)}, bf16[1024,768]{1,0:T(8,128)(2,1)}, u32[]{:S(2)}) copy-start(bf16[1024,768]{1,0:T(8,128)(2,1)} %reshape.557) | copy-start | bytes 4718596
  89.1 2.0 %copy-start.42 = (bf16[3,256,256]{2,1,0:T(8,128)(2,1)S(1)}, bf16[3,256,256]{2,1,0:T(8,128)(2,1)}, u32[]{:S(2)}) copy-start(bf16[3,256,256]{2,1,0:T(8,128)(2,1)} %get-tuple-element.109) | copy-start | bytes 1179652
  91.1 2.0 %copy-start.7 = (bf16[1024,768]{1,0:T(8,128)(2,1)S(1)}, bf16[1024,768]{1,0:T(8,128)(2,1)}, u32[]{:S(2)}) copy-start(bf16[1024,768]{1,0:T(8,128)(2,1)} %reshape.559) | copy-start | bytes 4718596
  91.1 2.0 %copy-start.41 = (bf16[3,256,256]{2,1,0:T(8,128)(2,1)S(1)}, bf16[3,256,256]{2,1,0:T(8,128)(2,1)}, u32[]{:S(2)}) copy-start(bf16[3,256,256]{2,1,0:T(8,128)(2,1)} %get-tuple-element.108) | copy-start | bytes 1179652
  93.1 1.4 %copy-start.8 = (bf16[1024,768]{1,0:T(8,128)(2,1)S(1)}, bf16[1024,768]{1,0:T(8,128)(2,1)}, u32[]{:S(2)}) copy-start(bf16[1024,768]{1,0:T(8,128)(2,1)} %reshape.561) | copy-start | bytes 4718596
  93.1 1.5 %copy-start.40 = (bf16[3,256,256]{2,1,0:T(8,128)(2,1)S(1)}, bf16[3,256,256]{2,1,0:T(8,128)(2,1)}, u32[]{:S(2)}) copy-start(bf16[3,256,256]{2,1,0:T(8,128)(2,1)} %get-tuple-element.107) | copy-start | bytes 1179652
  94.6 1.4 %copy-start.9 = (bf16[1024,768]{1,0:T(8,128)(2,1)S(1)}, bf16[1024,768]{1,0:T(8,128)(2,1)}, u32[]{:S(2)}) copy-start(bf16[1024,768]{1,0:T(8,128)(2,1)} %reshape.563) | copy-start | bytes 4718596
  94.6 1.5 %copy-start.39 = (bf16[3,256,256]{2,1,0:T(8,128)(2,1)S(1)}, bf16[3,256,256]{2,1,0:T(8,128)(2,1)}, u32[]{:S(2)}) copy-start(bf16[3,256,256]{2,1,0:T(8,128)(2,1)} %get-tuple-element.106) | copy-start | bytes 1179652
  96.0 1.4 %copy-start.10 = (bf16[1024,768]{1,0:T(8,128)(2,1)S(1)}, bf16[1024,768]{1,0:T(8,128)(2,1)}, u32[]{:S(2)}) copy-start(bf16[1024,768]{1,0:T(8,128)(2,1)} %reshape.565) | copy-start | bytes 4718596
  96.0 1.5 %copy-start.38 = (bf16[3,256,256]{2,1,0:T(8,128)(2,1)S(1)}, bf16[3,256,256]{2,1,0:T(8,128)(2,1)}, u32[]{:S(2)}) copy-start(bf16[3,256,256]{2,1,0:T(8,128)(2,1)} %get-tuple-element.105) | copy-start | bytes 1179652
  97.5 1.4 %copy-start.11 = (bf16[1024,768]{1,0:T(8,128)(2,1)S(1)}, bf16[1024,768]{1,0:T(8,128)(2,1)}, u32[]{:S(2)}) copy-start(bf16[1024,768]{1,0:T(8,128)(2,1)} %reshape.567) | copy-start | bytes 4718596
  97.5 1.5 %copy-start.37 = (bf16[3,256,256]{2,1,0:T(8,128)(2,1)S(1)}, bf16[3,256,256]{2,1,0:T(8,128)(2,1)}, u32[]{:S(2)}) copy-start(bf16[3,256,256]{2,1,0:T(8,128)(2,1)} %get-tuple-element.112) | copy-start | bytes 1179652
  99.5 3.4 %copy-start.35 = (bf16[1024,768]{1,0:T(8,128)(2,1)S(1)}, bf16[1024,768]{1,0:T(8,128)(2,1)}, u32[]{:S(2)}) copy-start(bf16[1024,768]{1,0:T(8,128)(2,1)} %reshape.569) | copy-start | bytes 4718596
  99.6 3.4 %copy-start.47 = (bf16[3,256,256]{2,1,0:T(8,128)(2,1)S(1)}, bf16[3,256,256]{2,1,0:T(8,128)(2,1)}, u32[]{:S(2)}) copy-start(bf16[3,256,256]{2,1,0:T(8,128)(2,1)} %get-tuple-element.104) | copy-start | bytes 1179652
  99.6 3.4 %copy-start.50 = (f32[256]{0:T(256)S(1)}, f32[256]{0:T(256)}, u32[]{:S(2)}) copy-start(f32[256]{0:T(256)} %param.34) | copy-start | bytes 3076
  103.0 2.2 %copy-start.1 = (bf16[16,64,256]{2,1,0:T(8,128)(2,1)S(1)}, bf16[16,64,256]{2,1,0:T(8,128)(2,1)}, u32[]{:S(2)}) copy-start(bf16[16,64,256]{2,1,0:T(8,128)(2,1)} %param.29) | copy-start | bytes 1572868
where the time goes:
time: 107 us; the launch traced here: 105 us
  local copies, waits for them, and re-layouts  62.4 us (58%)
  starting transfers between devices  18.3 us (17%)
  other arithmetic  13.4 us (13%)
  matrix products  10.3 us (10%)
    reshape x9, local copies, waits for them, and re-layouts, per_device(): joined = jnp.concatenate(windows, axis=-1).reshape(-1, 3 * channels)  18.7 us
    unnamed x108, local copies, waits for them, and re-layouts  15.3 us
    concatenate x9, local copies, waits for them, and re-layouts, per_device(): joined = jnp.concatenate(windows, axis=-1).reshape(-1, 3 * channels)  10.9 us
    dot_general x9, matrix products, per_device(): jnp.dot(joined, weight_rows, preferred_element_type=jnp.float32)  9.09 us
    concatenate x9, other arithmetic, per_device(): joined = jnp.concatenate(windows, axis=-1).reshape(-1, 3 * channels)  7.17 us
    all_to_all x1, starting transfers between devices, per_device(): lax.all_to_all(outgoing, 'blk', split_axis=0, concat_axis=0, tiled=True)  6.54 us
    all_to_all x1, starting transfers between devices, per_device(): lax.all_to_all(replies, 'blk', split_axis=0, concat_axis=0, tiled=True)  6.15 us
    gather x6, local copies, waits for them, and re-layouts, pick_layers(): jnp.take(source_layers, jnp.clip(slots, 0, source_layers.shape[0] - 1), a...  5.77 us
  transfers between devices with their start and end apart: 4, of which 0 were waited for; matrix products, arithmetic and copies ran while one was open for 61% of the time, Pallas kernels for 0%

commit v1 on v0

v1 whole, which is shorter than its diff:
```python
import functools

import jax
import jax.numpy as jnp
from jax import lax
from jax.experimental import pallas as pl
from jax.experimental.pallas import tpu as pltpu
from jax.sharding import PartitionSpec as P

EDGE = 4
LAYER = EDGE * EDGE
VOX = EDGE * LAYER
PLANE = 4
LANES = 128
HBM = pl.BlockSpec(memory_space=pl.ANY)
VMEM = pl.BlockSpec(memory_space=pltpu.VMEM)
SMEM = pl.BlockSpec(memory_space=pltpu.SMEM)


def near(array):
    return pltpu.with_memory_space_constraint(array, pltpu.VMEM)


def far(array):
    return pltpu.with_memory_space_constraint(array, pltpu.HBM)


def cost(flops, moved):
    return pl.CostEstimate(flops=flops, bytes_accessed=moved, transcendentals=0)


def occupied(occ, layer, channels):
    slots = occ.shape[0]
    shape = (LAYER, slots, VOX)
    voxel = lax.broadcasted_iota(jnp.int32, shape, 0) + layer * LAYER
    column = lax.broadcasted_iota(jnp.int32, shape, 2)
    picked = jnp.where(voxel == column, jnp.broadcast_to(occ[None], shape), 0.0)
    picked = picked.astype(jnp.bfloat16).reshape(LAYER * slots, VOX)
    ones = jnp.ones((VOX, channels), jnp.bfloat16)
    return jnp.dot(picked, ones, preferred_element_type=jnp.float32)


def params(mib):
    return pltpu.CompilerParams(vmem_limit_bytes=mib * 1024 * 1024)


def start_all(pairs, sems):
    copies = [pltpu.make_async_copy(src, dst, sems.at[i]) for i, (src, dst) in enumerate(pairs)]
    for copy in copies:
        copy.start()
    return copies


def prepare_kernel(
    features, occupancy, previous, after, cube, core, next_, own, values_in, occ_in, sems
):
    slots, _, channels = features.shape
    rows = LAYER * slots
    copies = start_all(((features, values_in), (occupancy, occ_in), (previous, own)), sems)
    row = lax.broadcasted_iota(jnp.int32, (rows, rows), 0)
    column = lax.broadcasted_iota(jnp.int32, (rows, rows), 1)
    swap = (row // slots == column % LAYER) & (row % slots == column // LAYER)
    swap = jnp.where(swap, 1.0, 0.0).astype(jnp.bfloat16)
    even = lax.rem(lax.axis_index("blk"), 2) == 0
    copies[1].wait()
    occ = occ_in[...].astype(jnp.float32)
    copies[0].wait()
    for layer in range(EDGE):
        span = pl.ds(layer * LAYER, LAYER)
        values = values_in[:, span, :].reshape(rows, channels)
        turned = jnp.dot(swap, values, preferred_element_type=jnp.float32)
        turned = turned * occupied(occ, layer, channels)
        cube[span] = turned.astype(jnp.bfloat16).reshape(LAYER, slots, channels)
    first, last = pl.ds(0, LAYER), pl.ds(VOX - LAYER, LAYER)

    @pl.when(even)
    def _():
        core[...] = cube[last]
        next_[...] = cube[first]

    @pl.when(jnp.logical_not(even))
    def _():
        core[...] = cube[first]
        next_[...] = cube[last]

    copies[2].wait()


def conv_kernel(
    cube, core, next_, near_t, occupancy, weight, scale, shift, after, hidden,
    volume, taps, total, near_in, occ_in, scale_in, shift_in, sems,
):
    slots, channels = cube.shape[1], cube.shape[2]
    rows = LAYER * slots
    side = EDGE + 2
    copies = start_all(
        [(near_t, near_in), (occupancy, occ_in), (scale, scale_in), (shift, shift_in)]
        + [(weight.at[pl.ds(9 * a, 9)], taps.at[pl.ds(9 * a, 9)]) for a in range(3)],
        sems,
    )
    even = lax.rem(lax.axis_index("blk"), 2) == 0
    volume[...] = jnp.zeros(volume.shape, volume.dtype)
    inner = pl.ds(1, EDGE)
    cells = cube[...].reshape(EDGE, EDGE, EDGE, slots, channels)
    volume[inner, inner, inner] = cells

    row = lax.broadcasted_iota(jnp.int32, (rows, rows), 0)
    column = lax.broadcasted_iota(jnp.int32, (rows, rows), 1)
    same_place = row // slots == column // slots
    slot_of = (column % slots).astype(jnp.float32)
    spread = lax.broadcasted_iota(jnp.int32, (rows, slots), 0) % slots
    spread = spread == lax.broadcasted_iota(jnp.int32, (rows, slots), 1)
    spread = jnp.where(spread, 1.0, 0.0).astype(jnp.bfloat16)
    for copy in copies[:4]:
        copy.wait()
    near_rows = lax.dot_general(
        spread,
        near_in[...].astype(jnp.float32).astype(jnp.bfloat16),
        (((1,), (1,)), ((), ())),
        preferred_element_type=jnp.float32,
    )

    def gathered(face, layer):
        pick = same_place & (slot_of == near_rows[:, face : face + 1])
        pick = jnp.where(pick, 1.0, 0.0).astype(jnp.bfloat16)
        layer = layer.reshape(rows, channels)
        out = jnp.dot(pick, layer, preferred_element_type=jnp.float32).astype(jnp.bfloat16)
        return out.reshape(EDGE, EDGE, slots, channels)

    @pl.when(even)
    def _():
        volume[0, inner, inner] = gathered(0, next_[...])
        volume[EDGE + 1, inner, inner] = gathered(1, core[...])

    @pl.when(jnp.logical_not(even))
    def _():
        volume[0, inner, inner] = gathered(0, core[...])
        volume[EDGE + 1, inner, inner] = gathered(1, next_[...])

    last = EDGE - 1
    volume[inner, 0, inner] = gathered(2, cells[:, last])
    volume[inner, EDGE + 1, inner] = gathered(3, cells[:, 0])
    volume[inner, inner, 0] = gathered(4, cells[:, :, last])
    volume[inner, inner, EDGE + 1] = gathered(5, cells[:, :, 0])

    occ = occ_in[...].astype(jnp.float32)
    for a in range(3):
        copies[4 + a].wait()
        for x in range(EDGE):
            windows = [
                volume[x + a, pl.ds(b, EDGE), pl.ds(c, EDGE)].reshape(rows, channels)
                for b in range(3)
                for c in range(3)
            ]
            joined = jnp.concatenate(windows, axis=1)
            kernel = taps[pl.ds(9 * a, 9)].reshape(9 * channels, channels)
            part = jnp.dot(joined, kernel, preferred_element_type=jnp.float32)
            span = pl.ds(x * rows, rows)
            if a == 2:
                full = occupied(occ, x, LANES)
            for h in range(channels // LANES):
                lanes = slice(h * LANES, (h + 1) * LANES)
                if a == 0:
                    total[h, span] = part[:, lanes]
                elif a == 1:
                    total[h, span] += part[:, lanes]
                else:
                    out = (total[h, span] + part[:, lanes]) * scale_in[:, lanes] + shift_in[:, lanes]
                    total[h, span] = jnp.where(full > 0.5, jnp.maximum(out, 0.0), -1.0)
    for x in range(EDGE):
        for slot in range(slots):
            for h in range(channels // LANES):
                hidden[slot, pl.ds(x * LAYER, LAYER), pl.ds(h * LANES, LANES)] = total[
                    h, pl.ds(x * rows + slot, LAYER, stride=slots), :
                ]


def ask_kernel(first, second, planes, old_owner, old_slot, *refs):
    steps = planes - 1
    asks, plan = refs[:steps], refs[steps]
    queue, used = refs[steps + 1 :]
    slots = old_slot.shape[0]
    me = lax.axis_index("blk")
    width = first + second

    def clear(i, _):
        queue[i] = 0
        plan[i] = slots
        return 0

    lax.fori_loop(0, planes * width, clear, 0)
    for k in range(planes):
        used[k] = 0
        used[planes + k] = 0

    def place(s, _):
        owner = old_owner[s]
        side = lax.bitwise_and(lax.bitwise_xor(owner, me), PLANE - 1)
        block = side * slots + old_slot[s]
        step = lax.rem(me // PLANE - owner // PLANE + planes, planes)
        n_first, n_second = used[step], used[planes + step]
        early = (side < 2) & (n_first < first)
        at = step * width + jnp.where(early, n_first, first + n_second)
        used[step] = jnp.where(early, n_first + 1, n_first)
        used[planes + step] = jnp.where(early, n_second, n_second + 1)
        queue[at] = block
        plan[at] = s
        return 0

    lax.fori_loop(0, slots, place, 0)
    for i in range(width):
        plan[planes * width + i] = queue[i]
        for k in range(1, planes):
            asks[k - 1][i] = queue[k * width + i]


def pack_kernel(begin, count, steps, pools_n, *refs):
    asks, pools, refs = refs[:steps], refs[steps : steps + pools_n], refs[steps + pools_n :]
    outs, lists, sems = refs[-steps - 2 : -2], refs[-2], refs[-1]
    slots = pools[0].shape[0]
    copies = start_all([(asks[k], lists.at[k]) for k in range(steps)], sems)
    for k in range(steps):
        copies[k].wait()
        for i in range(count):
            block = lists[k, begin + i]
            for p, pool in enumerate(pools):
                @pl.when(block // slots == p)
                def _():
                    outs[k][i] = pool[lax.rem(block, slots)]


def pack(asks, pools, begin, count, after=()):
    block = pools[0].shape[1:]
    dtype = pools[0].dtype
    steps = len(asks)
    return pl.pallas_call(
        functools.partial(pack_kernel, begin, count, steps, len(pools)),
        out_shape=[pltpu.VMEM((count,) + block, dtype)] * steps,
        in_specs=[VMEM] * steps + [VMEM] * len(pools) + [HBM] * len(after),
        out_specs=[VMEM] * steps,
        scratch_shapes=[
            pltpu.SMEM((steps,) + asks[0].shape, jnp.int32),
            pltpu.SemaphoreType.DMA((steps,)),
        ],
        compiler_params=params(1),
        cost_estimate=cost(0, 3000000),
    )(*map(near, asks), *map(near, pools), *after)


def finish_kernel(first, second, steps, plan, hidden, weight, *refs):
    pools = refs[:PLANE]
    early, late = refs[PLANE : PLANE + steps], refs[PLANE + steps : PLANE + 2 * steps]
    out, moved, merged, plan_in, weight_in, sems = refs[PLANE + 2 * steps :]
    slots = out.shape[0]
    width = first + second
    copies = start_all(((plan, plan_in), (weight, weight_in)), sems)
    copies[0].wait()
    for i in range(width):
        block = plan_in[(steps + 1) * width + i]
        for p, pool in enumerate(pools):
            @pl.when(block // slots == p)
            def _():
                moved[plan_in[i]] = pool[lax.rem(block, slots)]
    for k in range(steps):
        at = (k + 1) * width
        for i in range(first):
            moved[plan_in[at + i]] = early[k][i]
        for i in range(second):
            moved[plan_in[at + first + i]] = late[k][i]
    copies[1].wait()
    group = min(4, slots)
    sent = []
    for j, g in enumerate(range(0, slots, group)):
        span = pl.ds(g, group)
        values = moved[span].reshape(group * VOX, moved.shape[2])
        projected = jnp.dot(values, weight_in[...], preferred_element_type=jnp.float32)
        projected = projected.astype(jnp.bfloat16).astype(jnp.float32)
        base = hidden[span].reshape(group * VOX, hidden.shape[2])
        done = jnp.where(base < 0.0, 0.0, base + projected)
        merged[span] = done.astype(out.dtype).reshape(group, VOX, out.shape[2])
        sent.append(pltpu.make_async_copy(merged.at[span], out.at[span], sems.at[2 + j]))
        sent[-1].start()
    for copy in sent:
        copy.wait()


def per_device(
    features,
    occupancy,
    neighbors,
    previous,
    old_owner,
    old_slot,
    conv_weight,
    norm_scale,
    norm_shift,
    prev_weight,
):
    slots, _, channels = features.shape
    rows = LAYER * slots
    count = lax.axis_size("blk")
    planes = count // PLANE
    cap = max(2, 2 * slots // count)
    first, second = 2 * cap, 2 * cap
    steps = planes - 1
    width = first + second

    def beside(array, flip):
        return lax.ppermute(array, "blk", [(i, i ^ flip) for i in range(count)])

    def along(array, step):
        return lax.ppermute(array, "blk", [(i, (i + PLANE * step) % count) for i in range(count)])

    prev_y = beside(previous, 2)
    prev_c = beside(previous, 1)

    ints = lambda *shape: jax.ShapeDtypeStruct(shape, jnp.int32)
    *asks, plan = pl.pallas_call(
        functools.partial(ask_kernel, first, second, planes),
        out_shape=[ints(width)] * steps + [ints((planes + 1) * width)],
        in_specs=[SMEM] * 2,
        out_specs=[SMEM] * (steps + 1),
        scratch_shapes=[pltpu.SMEM((planes * width,), jnp.int32), pltpu.SMEM((2 * planes,), jnp.int32)],
        compiler_params=params(1),
        cost_estimate=cost(0, 2000),
    )(old_owner.reshape(slots), old_slot)
    asked = [along(ask, -k) for k, ask in enumerate(asks, 1)]

    near_block = lambda *shape: pltpu.VMEM(shape, jnp.bfloat16)
    cube, to_core, to_next, own = pl.pallas_call(
        prepare_kernel,
        out_shape=[
            near_block(VOX, slots, channels),
            near_block(LAYER, slots, channels),
            near_block(LAYER, slots, channels),
            near_block(*previous.shape),
        ],
        in_specs=[HBM] * 3 + [HBM],
        out_specs=[VMEM] * 4,
        scratch_shapes=[
            pltpu.VMEM(features.shape, features.dtype),
            pltpu.VMEM(occupancy.shape, occupancy.dtype),
            pltpu.SemaphoreType.DMA((3,)),
        ],
        compiler_params=params(4),
        cost_estimate=cost(2 * EDGE * rows * (rows + VOX) * channels, 5 * rows * channels * 4),
    )(far(features), far(occupancy), far(previous), plan)
    from_core = beside(to_core, 1)
    from_next = lax.ppermute(
        to_next,
        "blk",
        [pair for i in range(1, count - 1, 2) for pair in ((i, i + 1), (i + 1, i))],
    )

    early = pack(asked, [own, prev_c], 0, first)
    sent = [along(part, k) for k, part in enumerate(early, 1)]
    prev_yc = beside(lax.optimization_barrier((prev_y, early[0]))[0], 1)
    pools = [own, prev_c, prev_y, prev_yc]
    late = pack(asked, pools, first, second, [early[0], from_core, from_next])
    sent += [along(part, k) for k, part in enumerate(late, 1)]

    side = EDGE + 2
    hidden = pl.pallas_call(
        conv_kernel,
        out_shape=pltpu.VMEM((slots, VOX, channels), jnp.float32),
        in_specs=[VMEM] * 3 + [HBM] * 6,
        out_specs=VMEM,
        scratch_shapes=[
            pltpu.VMEM((side, side, side, slots, channels), jnp.bfloat16),
            pltpu.VMEM(conv_weight.shape, jnp.bfloat16),
            pltpu.VMEM((channels // LANES, EDGE * rows, LANES), jnp.float32),
            pltpu.VMEM((6, slots), jnp.int32),
            pltpu.VMEM(occupancy.shape, jnp.int32),
            pltpu.VMEM((1, channels), jnp.float32),
            pltpu.VMEM((1, channels), jnp.float32),
            pltpu.SemaphoreType.DMA((7,)),
        ],
        compiler_params=params(12),
        cost_estimate=cost(2 * 27 * EDGE * rows * channels * channels, 8000000),
    )(
        near(cube),
        near(from_core),
        near(from_next),
        far(neighbors.T),
        far(occupancy),
        far(conv_weight),
        far(norm_scale[None]),
        far(norm_shift[None]),
        late[0],
    )

    return pl.pallas_call(
        functools.partial(finish_kernel, first, second, steps),
        out_shape=jax.ShapeDtypeStruct((slots, VOX, channels), jnp.bfloat16),
        in_specs=[HBM, VMEM, HBM] + [VMEM] * (PLANE + 2 * steps),
        out_specs=HBM,
        scratch_shapes=[
            near_block(slots + 1, VOX, channels),
            near_block(slots, VOX, channels),
            pltpu.SMEM(((planes + 1) * width,), jnp.int32),
            near_block(channels, channels),
            pltpu.SemaphoreType.DMA((2 + -(-slots // 4),)),
        ],
        compiler_params=params(4),
        cost_estimate=cost(2 * VOX * slots * channels * channels, 3000000),
    )(far(plan), near(hidden), far(prev_weight), *map(near, (*pools, *sent)))


def solution(mesh):
    rows = ("grp", "blk")
    in_specs = (
        P(rows, None, None),
        P(rows, None),
        P(rows, None),
        P(rows, None, None),
        P(rows, None),
        P(rows),
        P(),
        P(),
        P(),
        P(),
    )
    return jax.shard_map(
        per_device, mesh=mesh, in_specs=in_specs, out_specs=P(rows, None, None), check_vma=False
    )
```

time: 107 us -> 47.4 us (0.44); the launches traced: 105 us -> 47.2 us
  local copies, waits for them, and re-layouts: 62.4 us -> 1.31 us
  waiting for transfers between devices: 0.01 us -> 14 us
  other arithmetic: 13.4 us -> 0 us
  Pallas kernels: 0 us -> 13.1 us
  matrix products: 10.3 us -> 0 us
    reshape x9 -> x0, local copies, waits for them, and re-layouts: 18.7 us -> none  [per_device(): joined = jnp.concatenate(windows, axis=-1).reshape(-1, 3 * channels)]
    unnamed x108 -> x6, local copies, waits for them, and re-layouts: 15.3 us -> 1.31 us
    ppermute x2 -> x14, waiting for transfers between devices: 0.01 us -> 14 us  [the longest x9 11.2 us: along(): lax.ppermute(array, 'blk', [(i, (i + PLANE * step) % count) for i in rang...]
    pallas_call x0 -> x6, Pallas kernels: none -> 13.1 us  [the longest x1 5.95 us: per_device(): pl.pallas_call(conv_kernel, out_shape=pltpu.VMEM((slots, VOX, channels),...]
    ppermute x2 -> x14, starting transfers between devices: 5.61 us -> 18.6 us  [the longest x9 12.4 us: along(): lax.ppermute(array, 'blk', [(i, (i + PLANE * step) % count) for i in rang...]
    all_to_all x2 -> x0, starting transfers between devices: 12.7 us -> none  [the longest x1 6.54 us: per_device(): lax.all_to_all(outgoing, 'blk', split_axis=0, concat_axis=0, tiled=True)]
    concatenate x9 -> x0, local copies, waits for them, and re-layouts: 10.9 us -> none  [per_device(): joined = jnp.concatenate(windows, axis=-1).reshape(-1, 3 * channels)]
    dot_general x10 -> x0, matrix products: 10.3 us -> none  [the longest x9 9.09 us: per_device(): jnp.dot(joined, weight_rows, preferred_element_type=jnp.float32)]
  transfers between devices with their start and end apart: 4 -> 14, of which waited for: 0 -> 5; matrix products, arithmetic and copies ran while one was open for 61% -> 0% of each run, Pallas kernels for 0% -> 23%
where the time goes in v1:
time: 47.4 us; the launch traced here: 47.2 us
  starting transfers between devices  18.6 us (39%)
  waiting for transfers between devices  14 us (30%)
  Pallas kernels  13.1 us (28%)
  local copies, waits for them, and re-layouts  1.31 us (3%)
    ppermute x9, starting transfers between devices, along(): lax.ppermute(array, 'blk', [(i, (i + PLANE * step) % count) for i in rang...  12.4 us
    ppermute x9, waiting for transfers between devices, along(): lax.ppermute(array, 'blk', [(i, (i + PLANE * step) % count) for i in rang...  11.2 us
    pallas_call x1, Pallas kernels, per_device(): pl.pallas_call(conv_kernel, out_shape=pltpu.VMEM((slots, VOX, channels),...  5.95 us
    ppermute x1, starting transfers between devices, per_device(): lax.ppermute(to_next, 'blk', [pair for i in range(1, count - 1, 2) for pa...  3.53 us
    ppermute x4, starting transfers between devices, beside(): return lax.ppermute(array, 'blk', [(i, i ^ flip) for i in range(count)])  2.7 us
    ppermute x4, waiting for transfers between devices, beside(): return lax.ppermute(array, 'blk', [(i, i ^ flip) for i in range(count)])  2.25 us
    pallas_call x1, Pallas kernels, per_device(): pl.pallas_call(functools.partial(finish_kernel, first, second, steps), ou...  2.06 us
    pallas_call x1, Pallas kernels, per_device(): pl.pallas_call(functools.partial(ask_kernel, first, second, planes), out_...  1.84 us
  transfers between devices with their start and end apart: 14, of which 5 were waited for; matrix products, arithmetic and copies ran while one was open for 0% of the time, Pallas kernels for 23%

profile of v1, /device:TPU:11, one launch (start us, length us, event | category | flops | bytes accessed | tf_op | source)
XLA Modules:
  0.0 47.2 jit_solution(10618890239304428800)
XLA Ops:
  0.0 0.7 %collective-permute-start.5 = (bf16[16,64,256]{2,1,0:T(8,128)(2,1)}, bf16[16,64,256]{2,1,0:T(8,128)(2,1)S(1)}, u32[]{:S(2)}, u32[]{:S(2)}) collective-permute-start(bf16[16,64,256]{2,1,0:T(8,128)(2,1)} %previous.1), channel_id=1, source_target_pairs={{0,1},{1,0},{2,3},{3,2},{4,5},{5,4},{6,7},{7,6},{8,9},{9,8},{10,11... | collective-permute-start | bytes 1572872 | tf_op jit(solution)/shard_map/ppermute | solution.py:309
  0.7 1.2 %collective-permute-start.6 = (bf16[16,64,256]{2,1,0:T(8,128)(2,1)}, bf16[16,64,256]{2,1,0:T(8,128)(2,1)S(1)}, u32[]{:S(2)}, u32[]{:S(2)}) collective-permute-start(bf16[16,64,256]{2,1,0:T(8,128)(2,1)} %previous.1), channel_id=1, source_target_pairs={{0,2},{1,3},{2,0},{3,1},{4,6},{5,7},{6,4},{7,5},{8,10},{9,11},{10,... | collective-permute-start | bytes 1572872 | tf_op jit(solution)/shard_map/ppermute | solution.py:309
  1.9 0.0 copy-start.1
  1.9 0.7 %copy-done.1 = s32[16,1]{0,1:T(1,128)S(1)} copy-done((s32[16,1]{0,1:T(1,128)S(1)}, s32[16,1]{0,1:T(1,128)}, u32[]{:S(2)}) %copy-start.1) | copy-done | bytes 88
  2.6 0.0 copy-start.2
  2.6 0.7 %copy-done.2 = s32[16]{0:T(128)S(1)} copy-done((s32[16]{0:T(128)S(1)}, s32[16]{0:T(128)}, u32[]{:S(2)}) %copy-start.2) | copy-done | bytes 88
  3.2 1.8 %shard_map.100 = (s32[8]{0:T(128)S(1)}, s32[8]{0:T(128)S(1)}, s32[8]{0:T(128)S(1)}, s32[40]{0:T(128)S(1)}) custom-call(s32[16]{0:T(128)S(1)} %bitcast.4, s32[16]{0:T(128)S(1)} %copy-done.2), custom_call_target="tpu_custom_call" | custom-call | bytes 2000 | tf_op jit(solution)/shard_map/pallas_call | solution.py:318
  5.1 0.0 copy-start
  5.1 0.2 collective-permute-start.2
  5.3 2.3 %collective-permute-start.3 = (s32[8]{0:T(128)S(1)}, s32[8]{0:T(128)S(1)}, u32[]{:S(2)}, u32[]{:S(2)}) collective-permute-start(s32[8]{0:T(128)S(1)} %get-tuple-element.25), channel_id=1, source_target_pairs={{0,8},{1,9},{2,10},{3,11},{4,12},{5,13},{6,14},{7,15},{8,0},{9,1},... | collective-permute-start | bytes 104 | tf_op jit(solution)/shard_map/ppermute | solution.py:312
  7.6 2.2 %collective-permute-start.4 = (s32[8]{0:T(128)S(1)}, s32[8]{0:T(128)S(1)}, u32[]{:S(2)}, u32[]{:S(2)}) collective-permute-start(s32[8]{0:T(128)S(1)} %get-tuple-element.26), channel_id=1, source_target_pairs={{0,4},{1,5},{2,6},{3,7},{4,8},{5,9},{6,10},{7,11},{8,12},{9,13},{1... | collective-permute-start | bytes 104 | tf_op jit(solution)/shard_map/ppermute | solution.py:312
  9.8 1.5 %shard_map.101 = (bf16[64,16,256]{2,1,0:T(8,128)(2,1)S(1)}, bf16[16,16,256]{2,1,0:T(8,128)(2,1)S(1)}, bf16[16,16,256]{2,1,0:T(8,128)(2,1)S(1)}, bf16[16,64,256]{2,1,0:T(8,128)(2,1)S(1)}) custom-call(bf16[16,64,256]{2,1,0:T(8,128)(2,1)} %features.1, s32[16,64]{1,0:T(8,128)} %occupancy.3, bf16[16,64,256]{2,1,0:T(8,128)(2,1)} %previous.1, ...), custom_call_target="tpu_custom_call" | custom-call | flops 167772160 | bytes 1310720 | tf_op jit(solution)/shard_map/pallas_call | solution.py:330
  11.3 0.0 collective-permute-done.2.refs_0_
  11.3 0.0 collective-permute-done.3.refs_1_
  11.3 0.0 collective-permute-done.4.refs_2_
  11.4 0.0 collective-permute-done.5.refs_4_.refs_1_
  11.4 0.8 %shard_map.102 = (bf16[4,64,256]{2,1,0:T(8,128)(2,1)S(1)}, bf16[4,64,256]{2,1,0:T(8,128)(2,1)S(1)}, bf16[4,64,256]{2,1,0:T(8,128)(2,1)S(1)}) custom-call(s32[8]{0:T(128)S(1)} %collective-permute-done.2.refs_0_, s32[8]{0:T(128)S(1)} %collective-permute-done.3.refs_1_, s32[8]{0:T(128)S(1)} %collective-permute-done.4.refs_2_, ...), custom_call_target="tpu_custom_call" | custom-call | bytes 3000000 | tf_op jit(solution)/shard_map/pallas_call | solution.py:236
  12.2 2.2 %collective-permute-done.6.refs_5_.refs_2_ = bf16[16,64,256]{2,1,0:T(8,128)(2,1)S(1)} collective-permute-done((bf16[16,64,256]{2,1,0:T(8,128)(2,1)}, bf16[16,64,256]{2,1,0:T(8,128)(2,1)S(1)}, u32[]{:S(2)}, u32[]{:S(2)}) %collective-permute-start.6) | collective-permute-done | bytes 524320 | tf_op jit(solution)/shard_map/ppermute | solution.py:309
  14.4 0.8 %collective-permute-start.7 = (bf16[16,64,256]{2,1,0:T(8,128)(2,1)S(1)}, bf16[16,64,256]{2,1,0:T(8,128)(2,1)S(1)}, u32[]{:S(2)}, u32[]{:S(2)}) collective-permute-start(bf16[16,64,256]{2,1,0:T(8,128)(2,1)S(1)} %collective-permute-done.6.refs_5_.refs_2_), channel_id=1, source_target_pairs={{0,1},{1,0},{2,3},{3,2},{4,5},{5,4},{6,7},{7,6},{8,9},{9,8},{10,11... | collective-permute-start | bytes 1572872 | tf_op jit(solution)/shard_map/ppermute | solution.py:309
  15.2 0.0 collective-permute-start
  15.2 3.5 %collective-permute-start.1 = (bf16[16,16,256]{2,1,0:T(8,128)(2,1)S(1)}, bf16[16,16,256]{2,1,0:T(8,128)(2,1)S(1)}, u32[]{:S(2)}, u32[]{:S(2)}) collective-permute-start(bf16[16,16,256]{2,1,0:T(8,128)(2,1)S(1)} %get-tuple-element.23), channel_id=1, source_target_pairs={{1,2},{2,1},{3,4},{4,3},{5,6},{6,5},{7,8},{8,7},{9,10},{10,9},{11,... | collective-permute-start | bytes 393224 | tf_op jit(solution)/shard_map/ppermute | solution.py:349
  18.8 1.3 %collective-permute-start.8 = (bf16[4,64,256]{2,1,0:T(8,128)(2,1)S(1)}, bf16[4,64,256]{2,1,0:T(8,128)(2,1)S(1)}, u32[]{:S(2)}, u32[]{:S(2)}) collective-permute-start(bf16[4,64,256]{2,1,0:T(8,128)(2,1)S(1)} %get-tuple-element.28.refs_7_), channel_id=1, source_target_pairs={{0,4},{1,5},{2,6},{3,7},{4,8},{5,9},{6,10},{7,11},{8,12},{9,13},{1... | collective-permute-start | bytes 393224 | tf_op jit(solution)/shard_map/ppermute | solution.py:312
  20.1 0.2 collective-permute-start.10
  20.3 0.0 collective-permute-done.refs_8_.core
  20.3 2.3 %collective-permute-start.9 = (bf16[4,64,256]{2,1,0:T(8,128)(2,1)S(1)}, bf16[4,64,256]{2,1,0:T(8,128)(2,1)S(1)}, u32[]{:S(2)}, u32[]{:S(2)}) collective-permute-start(bf16[4,64,256]{2,1,0:T(8,128)(2,1)S(1)} %get-tuple-element.31), channel_id=1, source_target_pairs={{0,8},{1,9},{2,10},{3,11},{4,12},{5,13},{6,14},{7,15},{8,0},{9,1},... | collective-permute-start | bytes 393224 | tf_op jit(solution)/shard_map/ppermute | solution.py:312
  22.6 0.6 %collective-permute-done.1.refs_9_.next_ = bf16[16,16,256]{2,1,0:T(8,128)(2,1)S(1)} collective-permute-done((bf16[16,16,256]{2,1,0:T(8,128)(2,1)S(1)}, bf16[16,16,256]{2,1,0:T(8,128)(2,1)S(1)}, u32[]{:S(2)}, u32[]{:S(2)}) %collective-permute-start.1) | collective-permute-done | bytes 131104 | tf_op jit(solution)/shard_map/ppermute | solution.py:349
  23.2 0.0 collective-permute-done.7.refs_6_.refs_3_
  23.2 0.9 %shard_map.103 = (bf16[4,64,256]{2,1,0:T(8,128)(2,1)S(1)}, bf16[4,64,256]{2,1,0:T(8,128)(2,1)S(1)}, bf16[4,64,256]{2,1,0:T(8,128)(2,1)S(1)}) custom-call(s32[8]{0:T(128)S(1)} %collective-permute-done.2.refs_0_, s32[8]{0:T(128)S(1)} %collective-permute-done.3.refs_1_, s32[8]{0:T(128)S(1)} %collective-permute-done.4.refs_2_, ...), custom_call_target="tpu_custom_call" | custom-call | bytes 3000000 | tf_op jit(solution)/shard_map/pallas_call | solution.py:236
  24.2 1.3 %collective-permute-start.11 = (bf16[4,64,256]{2,1,0:T(8,128)(2,1)S(1)}, bf16[4,64,256]{2,1,0:T(8,128)(2,1)S(1)}, u32[]{:S(2)}, u32[]{:S(2)}) collective-permute-start(bf16[4,64,256]{2,1,0:T(8,128)(2,1)S(1)} %get-tuple-element.30.after), channel_id=1, source_target_pairs={{0,4},{1,5},{2,6},{3,7},{4,8},{5,9},{6,10},{7,11},{8,12},{9,13},{1... | collective-permute-start | bytes 393224 | tf_op jit(solution)/shard_map/ppermute | solution.py:312
  25.5 1.1 %collective-permute-start.12 = (bf16[4,64,256]{2,1,0:T(8,128)(2,1)S(1)}, bf16[4,64,256]{2,1,0:T(8,128)(2,1)S(1)}, u32[]{:S(2)}, u32[]{:S(2)}) collective-permute-start(bf16[4,64,256]{2,1,0:T(8,128)(2,1)S(1)} %get-tuple-element.33), channel_id=1, source_target_pairs={{0,8},{1,9},{2,10},{3,11},{4,12},{5,13},{6,14},{7,15},{8,0},{9,1},... | collective-permute-start | bytes 393224 | tf_op jit(solution)/shard_map/ppermute | solution.py:312
  26.6 0.0 collective-permute-done.8.refs_4_
  26.6 1.4 %collective-permute-start.13 = (bf16[4,64,256]{2,1,0:T(8,128)(2,1)S(1)}, bf16[4,64,256]{2,1,0:T(8,128)(2,1)S(1)}, u32[]{:S(2)}, u32[]{:S(2)}) collective-permute-start(bf16[4,64,256]{2,1,0:T(8,128)(2,1)S(1)} %get-tuple-element.34), channel_id=1, source_target_pairs={{0,12},{1,13},{2,14},{3,15},{4,0},{5,1},{6,2},{7,3},{8,4},{9,5},{1... | collective-permute-start | bytes 393224 | tf_op jit(solution)/shard_map/ppermute | solution.py:312
  28.0 5.9 %shard_map.104.hidden = f32[16,64,256]{2,1,0:T(8,128)S(1)} custom-call(bf16[64,16,256]{2,1,0:T(8,128)(2,1)S(1)} %get-tuple-element.21.cube, bf16[16,16,256]{2,1,0:T(8,128)(2,1)S(1)} %collective-permute-done.refs_8_.core, bf16[16,16,256]{2,1,0:T(8,128)(2,1)S(1)} %collective-permute-done.1.refs_9_.next_, s32[6,16]{1,0:T(8,128)} %bitcast.5, ...), custom_call_target="tpu_custom_call" | custom-call | flops 3623878656 | bytes 8000000 | tf_op jit(solution)/shard_map/pallas_call | solution.py:363
  33.9 0.0 copy-done
  34.0 0.0 collective-permute-done.10.refs_6_
  34.0 0.0 collective-permute-done.9.refs_5_
  34.0 6.1 %collective-permute-done.11.refs_7_ = bf16[4,64,256]{2,1,0:T(8,128)(2,1)S(1)} collective-permute-done((bf16[4,64,256]{2,1,0:T(8,128)(2,1)S(1)}, bf16[4,64,256]{2,1,0:T(8,128)(2,1)S(1)}, u32[]{:S(2)}, u32[]{:S(2)}) %collective-permute-start.11) | collective-permute-done | bytes 131104 | tf_op jit(solution)/shard_map/ppermute | solution.py:312
  40.1 2.8 %collective-permute-done.12.refs_8_ = bf16[4,64,256]{2,1,0:T(8,128)(2,1)S(1)} collective-permute-done((bf16[4,64,256]{2,1,0:T(8,128)(2,1)S(1)}, bf16[4,64,256]{2,1,0:T(8,128)(2,1)S(1)}, u32[]{:S(2)}, u32[]{:S(2)}) %collective-permute-start.12) | collective-permute-done | bytes 131104 | tf_op jit(solution)/shard_map/ppermute | solution.py:312
  42.9 2.2 %collective-permute-done.13.refs_9_ = bf16[4,64,256]{2,1,0:T(8,128)(2,1)S(1)} collective-permute-done((bf16[4,64,256]{2,1,0:T(8,128)(2,1)S(1)}, bf16[4,64,256]{2,1,0:T(8,128)(2,1)S(1)}, u32[]{:S(2)}, u32[]{:S(2)}) %collective-permute-start.13) | collective-permute-done | bytes 131104 | tf_op jit(solution)/shard_map/ppermute | solution.py:312
  45.1 2.1 %shard_map.105 = bf16[16,64,256]{2,1,0:T(8,128)(2,1)} custom-call(s32[40]{0:T(128)} %copy-done, f32[16,64,256]{2,1,0:T(8,128)S(1)} %shard_map.104.hidden, bf16[256,256]{1,0:T(8,128)(2,1)} %weight.3, bf16[16,64,256]{2,1,0:T(8,128)(2,1)S(1)} %get-tuple-element.27.refs_3_.refs_0_, bf16[16,64,256]{2,1,0:T(8,128)(2,1)S(1)} %collective-permute-done.5.refs_4_.refs_1_, ...), custom_call_target="tpu_custom_call" | custom-call | flops 134217728 | bytes 3000000 | tf_op jit(solution)/shard_map/pallas_call | solution.py:392
Async XLA Ops:
  0.0 11.4 %collective-permute-start.5 = (bf16[16,64,256]{2,1,0:T(8,128)(2,1)}, bf16[16,64,256]{2,1,0:T(8,128)(2,1)S(1)}, u32[]{:S(2)}, u32[]{:S(2)}) collective-permute-start(bf16[16,64,256]{2,1,0:T(8,128)(2,1)} %previous.1), channel_id=1, source_target_pairs={{0,1},{1,0},{2,3},{3,2},{4,5},{5,4},{6,7},{7,6},{8,9},{9,8},{10,11... | collective-permute-start | bytes 1572872 | tf_op jit(solution)/shard_map/ppermute | solution.py:309
  0.7 13.8 %collective-permute-start.6 = (bf16[16,64,256]{2,1,0:T(8,128)(2,1)}, bf16[16,64,256]{2,1,0:T(8,128)(2,1)S(1)}, u32[]{:S(2)}, u32[]{:S(2)}) collective-permute-start(bf16[16,64,256]{2,1,0:T(8,128)(2,1)} %previous.1), channel_id=1, source_target_pairs={{0,2},{1,3},{2,0},{3,1},{4,6},{5,7},{6,4},{7,5},{8,10},{9,11},{10,... | collective-permute-start | bytes 1572872 | tf_op jit(solution)/shard_map/ppermute | solution.py:309
  1.9 0.7 %copy-start.1 = (s32[16,1]{0,1:T(1,128)S(1)}, s32[16,1]{0,1:T(1,128)}, u32[]{:S(2)}) copy-start(s32[16,1]{0,1:T(1,128)} %param.14) | copy-start | bytes 196
  2.6 0.7 %copy-start.2 = (s32[16]{0:T(128)S(1)}, s32[16]{0:T(128)}, u32[]{:S(2)}) copy-start(s32[16]{0:T(128)} %old_slot.1) | copy-start | bytes 196
  5.1 28.9 %copy-start = (s32[40]{0:T(128)}, s32[40]{0:T(128)S(1)}, u32[]{:S(2)}) copy-start(s32[40]{0:T(128)S(1)} %get-tuple-element.20.after.plan) | copy-start | bytes 484
  5.1 6.2 %collective-permute-start.2 = (s32[8]{0:T(128)S(1)}, s32[8]{0:T(128)S(1)}, u32[]{:S(2)}, u32[]{:S(2)}) collective-permute-start(s32[8]{0:T(128)S(1)} %get-tuple-element.24), channel_id=1, source_target_pairs={{0,12},{1,13},{2,14},{3,15},{4,0},{5,1},{6,2},{7,3},{8,4},{9,5},{1... | collective-permute-start | bytes 104 | tf_op jit(solution)/shard_map/ppermute | solution.py:312
  5.3 6.0 %collective-permute-start.3 = (s32[8]{0:T(128)S(1)}, s32[8]{0:T(128)S(1)}, u32[]{:S(2)}, u32[]{:S(2)}) collective-permute-start(s32[8]{0:T(128)S(1)} %get-tuple-element.25), channel_id=1, source_target_pairs={{0,8},{1,9},{2,10},{3,11},{4,12},{5,13},{6,14},{7,15},{8,0},{9,1},... | collective-permute-start | bytes 104 | tf_op jit(solution)/shard_map/ppermute | solution.py:312
  7.6 3.7 %collective-permute-start.4 = (s32[8]{0:T(128)S(1)}, s32[8]{0:T(128)S(1)}, u32[]{:S(2)}, u32[]{:S(2)}) collective-permute-start(s32[8]{0:T(128)S(1)} %get-tuple-element.26), channel_id=1, source_target_pairs={{0,4},{1,5},{2,6},{3,7},{4,8},{5,9},{6,10},{7,11},{8,12},{9,13},{1... | collective-permute-start | bytes 104 | tf_op jit(solution)/shard_map/ppermute | solution.py:312
  14.4 8.8 %collective-permute-start.7 = (bf16[16,64,256]{2,1,0:T(8,128)(2,1)S(1)}, bf16[16,64,256]{2,1,0:T(8,128)(2,1)S(1)}, u32[]{:S(2)}, u32[]{:S(2)}) collective-permute-start(bf16[16,64,256]{2,1,0:T(8,128)(2,1)S(1)} %collective-permute-done.6.refs_5_.refs_2_), channel_id=1, source_target_pairs={{0,1},{1,0},{2,3},{3,2},{4,5},{5,4},{6,7},{7,6},{8,9},{9,8},{10,11... | collective-permute-start | bytes 1572872 | tf_op jit(solution)/shard_map/ppermute | solution.py:309
  15.2 5.1 %collective-permute-start = (bf16[16,16,256]{2,1,0:T(8,128)(2,1)S(1)}, bf16[16,16,256]{2,1,0:T(8,128)(2,1)S(1)}, u32[]{:S(2)}, u32[]{:S(2)}) collective-permute-start(bf16[16,16,256]{2,1,0:T(8,128)(2,1)S(1)} %get-tuple-element.22), channel_id=1, source_target_pairs={{0,1},{1,0},{2,3},{3,2},{4,5},{5,4},{6,7},{7,6},{8,9},{9,8},{10,11... | collective-permute-start | bytes 393224 | tf_op jit(solution)/shard_map/ppermute | solution.py:309
  15.2 8.0 %collective-permute-start.1 = (bf16[16,16,256]{2,1,0:T(8,128)(2,1)S(1)}, bf16[16,16,256]{2,1,0:T(8,128)(2,1)S(1)}, u32[]{:S(2)}, u32[]{:S(2)}) collective-permute-start(bf16[16,16,256]{2,1,0:T(8,128)(2,1)S(1)} %get-tuple-element.23), channel_id=1, source_target_pairs={{1,2},{2,1},{3,4},{4,3},{5,6},{6,5},{7,8},{8,7},{9,10},{10,9},{11,... | collective-permute-start | bytes 393224 | tf_op jit(solution)/shard_map/ppermute | solution.py:349
  18.8 7.8 %collective-permute-start.8 = (bf16[4,64,256]{2,1,0:T(8,128)(2,1)S(1)}, bf16[4,64,256]{2,1,0:T(8,128)(2,1)S(1)}, u32[]{:S(2)}, u32[]{:S(2)}) collective-permute-start(bf16[4,64,256]{2,1,0:T(8,128)(2,1)S(1)} %get-tuple-element.28.refs_7_), channel_id=1, source_target_pairs={{0,4},{1,5},{2,6},{3,7},{4,8},{5,9},{6,10},{7,11},{8,12},{9,13},{1... | collective-permute-start | bytes 393224 | tf_op jit(solution)/shard_map/ppermute | solution.py:312
  20.1 13.8 %collective-permute-start.10 = (bf16[4,64,256]{2,1,0:T(8,128)(2,1)S(1)}, bf16[4,64,256]{2,1,0:T(8,128)(2,1)S(1)}, u32[]{:S(2)}, u32[]{:S(2)}) collective-permute-start(bf16[4,64,256]{2,1,0:T(8,128)(2,1)S(1)} %get-tuple-element.32), channel_id=1, source_target_pairs={{0,12},{1,13},{2,14},{3,15},{4,0},{5,1},{6,2},{7,3},{8,4},{9,5},{1... | collective-permute-start | bytes 393224 | tf_op jit(solution)/shard_map/ppermute | solution.py:312
  20.3 13.7 %collective-permute-start.9 = (bf16[4,64,256]{2,1,0:T(8,128)(2,1)S(1)}, bf16[4,64,256]{2,1,0:T(8,128)(2,1)S(1)}, u32[]{:S(2)}, u32[]{:S(2)}) collective-permute-start(bf16[4,64,256]{2,1,0:T(8,128)(2,1)S(1)} %get-tuple-element.31), channel_id=1, source_target_pairs={{0,8},{1,9},{2,10},{3,11},{4,12},{5,13},{6,14},{7,15},{8,0},{9,1},... | collective-permute-start | bytes 393224 | tf_op jit(solution)/shard_map/ppermute | solution.py:312
  24.2 15.9 %collective-permute-start.11 = (bf16[4,64,256]{2,1,0:T(8,128)(2,1)S(1)}, bf16[4,64,256]{2,1,0:T(8,128)(2,1)S(1)}, u32[]{:S(2)}, u32[]{:S(2)}) collective-permute-start(bf16[4,64,256]{2,1,0:T(8,128)(2,1)S(1)} %get-tuple-element.30.after), channel_id=1, source_target_pairs={{0,4},{1,5},{2,6},{3,7},{4,8},{5,9},{6,10},{7,11},{8,12},{9,13},{1... | collective-permute-start | bytes 393224 | tf_op jit(solution)/shard_map/ppermute | solution.py:312
  25.5 17.4 %collective-permute-start.12 = (bf16[4,64,256]{2,1,0:T(8,128)(2,1)S(1)}, bf16[4,64,256]{2,1,0:T(8,128)(2,1)S(1)}, u32[]{:S(2)}, u32[]{:S(2)}) collective-permute-start(bf16[4,64,256]{2,1,0:T(8,128)(2,1)S(1)} %get-tuple-element.33), channel_id=1, source_target_pairs={{0,8},{1,9},{2,10},{3,11},{4,12},{5,13},{6,14},{7,15},{8,0},{9,1},... | collective-permute-start | bytes 393224 | tf_op jit(solution)/shard_map/ppermute | solution.py:312
  26.6 18.5 %collective-permute-start.13 = (bf16[4,64,256]{2,1,0:T(8,128)(2,1)S(1)}, bf16[4,64,256]{2,1,0:T(8,128)(2,1)S(1)}, u32[]{:S(2)}, u32[]{:S(2)}) collective-permute-start(bf16[4,64,256]{2,1,0:T(8,128)(2,1)S(1)} %get-tuple-element.34), channel_id=1, source_target_pairs={{0,12},{1,13},{2,14},{3,15},{4,0},{5,1},{6,2},{7,3},{8,4},{9,5},{1... | collective-permute-start | bytes 393224 | tf_op jit(solution)/shard_map/ppermute | solution.py:312

commit v2 on v1

--- a/solution.py
+++ b/solution.py
@@ -52,7 +52,7 @@
 
 
 def prepare_kernel(
-    features, occupancy, previous, after, cube, core, next_, own, values_in, occ_in, sems
+    features, occupancy, previous, after, after2, cube, core, next_, own, values_in, occ_in, sems
 ):
     slots, _, channels = features.shape
     rows = LAYER * slots
@@ -87,14 +87,15 @@
 
 
 def conv_kernel(
-    cube, core, next_, near_t, occupancy, weight, scale, shift, after, hidden,
-    volume, taps, total, near_in, occ_in, scale_in, shift_in, sems,
+    room, steps, cube, core, next_, own, other, near_t, occupancy, weight, scale, shift, plan, after, *refs
 ):
+    early = refs[:steps]
+    hidden, moved, volume, taps, total, near_in, occ_in, scale_in, shift_in, plan_in, sems = refs[steps:]
     slots, channels = cube.shape[1], cube.shape[2]
     rows = LAYER * slots
     side = EDGE + 2
     copies = start_all(
-        [(near_t, near_in), (occupancy, occ_in), (scale, scale_in), (shift, shift_in)]
+        [(near_t, near_in), (occupancy, occ_in), (scale, scale_in), (shift, shift_in), (plan, plan_in)]
         + [(weight.at[pl.ds(9 * a, 9)], taps.at[pl.ds(9 * a, 9)]) for a in range(3)],
         sems,
     )
@@ -111,7 +112,7 @@
     spread = lax.broadcasted_iota(jnp.int32, (rows, slots), 0) % slots
     spread = spread == lax.broadcasted_iota(jnp.int32, (rows, slots), 1)
     spread = jnp.where(spread, 1.0, 0.0).astype(jnp.bfloat16)
-    for copy in copies[:4]:
+    for copy in copies[:5]:
         copy.wait()
     near_rows = lax.dot_general(
         spread,
@@ -120,6 +121,11 @@
         preferred_element_type=jnp.float32,
     )
 
+    for i in range(room):
+        fill(moved.at[plan_in[i]], own, other, plan_in[2 * (steps + 1) * room + i])
+        for k in range(steps):
+            moved[plan_in[2 * (k + 1) * room + i]] = early[k][i]
+
     def gathered(face, layer):
         pick = same_place & (slot_of == near_rows[:, face : face + 1])
         pick = jnp.where(pick, 1.0, 0.0).astype(jnp.bfloat16)
@@ -145,7 +151,7 @@
 
     occ = occ_in[...].astype(jnp.float32)
     for a in range(3):
-        copies[4 + a].wait()
+        copies[5 + a].wait()
         for x in range(EDGE):
             windows = [
                 volume[x + a, pl.ds(b, EDGE), pl.ds(c, EDGE)].reshape(rows, channels)
@@ -175,13 +181,14 @@
                 ]
 
 
-def ask_kernel(first, second, planes, old_owner, old_slot, *refs):
+def ask_kernel(room, planes, owner_in, slot_in, *refs):
     steps = planes - 1
     asks, plan = refs[:steps], refs[steps]
-    queue, used = refs[steps + 1 :]
+    old_owner, old_slot, queue, used, sems = refs[steps + 1 :]
     slots = old_slot.shape[0]
+    width = 2 * room
+    copies = start_all(((owner_in, old_owner), (slot_in, old_slot)), sems)
     me = lax.axis_index("blk")
-    width = first + second
 
     def clear(i, _):
         queue[i] = 0
@@ -189,21 +196,18 @@
         return 0
 
     lax.fori_loop(0, planes * width, clear, 0)
-    for k in range(planes):
+    for k in range(2 * planes):
         used[k] = 0
-        used[planes + k] = 0
+    for copy in copies:
+        copy.wait()
 
     def place(s, _):
-        owner = old_owner[s]
-        side = lax.bitwise_and(lax.bitwise_xor(owner, me), PLANE - 1)
-        block = side * slots + old_slot[s]
-        step = lax.rem(me // PLANE - owner // PLANE + planes, planes)
-        n_first, n_second = used[step], used[planes + step]
-        early = (side < 2) & (n_first < first)
-        at = step * width + jnp.where(early, n_first, first + n_second)
-        used[step] = jnp.where(early, n_first + 1, n_first)
-        used[planes + step] = jnp.where(early, n_second, n_second + 1)
-        queue[at] = block
+        away = lax.bitwise_xor(old_owner[s], me)
+        chip = away // 2
+        n = used[chip]
+        used[chip] = n + 1
+        at = chip * room + n
+        queue[at] = lax.bitwise_and(away, 1) * slots + old_slot[s]
         plan[at] = s
         return 0
 
@@ -214,59 +218,50 @@
             asks[k - 1][i] = queue[k * width + i]
 
 
-def pack_kernel(begin, count, steps, pools_n, *refs):
-    asks, pools, refs = refs[:steps], refs[steps : steps + pools_n], refs[steps + pools_n :]
-    outs, lists, sems = refs[-steps - 2 : -2], refs[-2], refs[-1]
-    slots = pools[0].shape[0]
-    copies = start_all([(asks[k], lists.at[k]) for k in range(steps)], sems)
+def fill(out, own, other, block):
+    slots = own.shape[0]
+
+    @pl.when(block < slots)
+    def _():
+        out[...] = own[block]
+
+    @pl.when(block >= slots)
+    def _():
+        out[...] = other[block - slots]
+
+
+def same_kernel(room, steps, plan, own, other, *refs):
+    asks, outs = refs[:steps], refs[steps : 2 * steps]
+    lists, asks_in, plan_in, sems = refs[2 * steps :]
+    copies = start_all([(asks[k], asks_in.at[k]) for k in range(steps)] + [(plan, plan_in)], sems)
     for k in range(steps):
         copies[k].wait()
-        for i in range(count):
-            block = lists[k, begin + i]
-            for p, pool in enumerate(pools):
-                @pl.when(block // slots == p)
-                def _():
-                    outs[k][i] = pool[lax.rem(block, slots)]
-
-
-def pack(asks, pools, begin, count, after=()):
-    block = pools[0].shape[1:]
-    dtype = pools[0].dtype
-    steps = len(asks)
-    return pl.pallas_call(
-        functools.partial(pack_kernel, begin, count, steps, len(pools)),
-        out_shape=[pltpu.VMEM((count,) + block, dtype)] * steps,
-        in_specs=[VMEM] * steps + [VMEM] * len(pools) + [HBM] * len(after),
-        out_specs=[VMEM] * steps,
-        scratch_shapes=[
-            pltpu.SMEM((steps,) + asks[0].shape, jnp.int32),
-            pltpu.SemaphoreType.DMA((steps,)),
-        ],
-        compiler_params=params(1),
-        cost_estimate=cost(0, 3000000),
-    )(*map(near, asks), *map(near, pools), *after)
-
-
-def finish_kernel(first, second, steps, plan, hidden, weight, *refs):
-    pools = refs[:PLANE]
-    early, late = refs[PLANE : PLANE + steps], refs[PLANE + steps : PLANE + 2 * steps]
-    out, moved, merged, plan_in, weight_in, sems = refs[PLANE + 2 * steps :]
+        for i in range(room):
+            fill(outs[k].at[i], own, other, asks_in[k, i])
+            lists[(k + 1) * room + i] = asks_in[k, room + i]
+    copies[steps].wait()
+    for i in range(room):
+        lists[i] = plan_in[2 * (steps + 1) * room + room + i]
+
+
+def cross_kernel(room, planes, lists, own, other, after, *refs):
+    outs, lists_in, sems = refs[:planes], *refs[planes:]
+    copies = start_all(((lists, lists_in),), sems)
+    copies[0].wait()
+    for k in range(planes):
+        for i in range(room):
+            fill(outs[k].at[i], own, other, lists_in[k * room + i])
+
+
+def finish_kernel(room, planes, plan, hidden, weight, gathered, *refs):
+    cross = refs[:planes]
+    out, moved, merged, plan_in, weight_in, sems = refs[planes:]
     slots = out.shape[0]
-    width = first + second
     copies = start_all(((plan, plan_in), (weight, weight_in)), sems)
     copies[0].wait()
-    for i in range(width):
-        block = plan_in[(steps + 1) * width + i]
-        for p, pool in enumerate(pools):
-            @pl.when(block // slots == p)
-            def _():
-                moved[plan_in[i]] = pool[lax.rem(block, slots)]
-    for k in range(steps):
-        at = (k + 1) * width
-        for i in range(first):
-            moved[plan_in[at + i]] = early[k][i]
-        for i in range(second):
-            moved[plan_in[at + first + i]] = late[k][i]
+    for k in range(planes):
+        for i in range(room):
+            moved[plan_in[(2 * k + 1) * room + i]] = cross[k][i]
     copies[1].wait()
     group = min(4, slots)
     sent = []
@@ -300,42 +295,47 @@
     rows = LAYER * slots
     count = lax.axis_size("blk")
     planes = count // PLANE
-    cap = max(2, 2 * slots // count)
-    first, second = 2 * cap, 2 * cap
     steps = planes - 1
-    width = first + second
-
-    def beside(array, flip):
+    room = 2 * max(2, 2 * slots // count)
+    width = 2 * room
+
+    def swap(array, flip):
         return lax.ppermute(array, "blk", [(i, i ^ flip) for i in range(count)])
 
-    def along(array, step):
-        return lax.ppermute(array, "blk", [(i, (i + PLANE * step) % count) for i in range(count)])
-
-    prev_y = beside(previous, 2)
-    prev_c = beside(previous, 1)
-
-    ints = lambda *shape: jax.ShapeDtypeStruct(shape, jnp.int32)
+    def ints(*shape):
+        return jax.ShapeDtypeStruct(shape, jnp.int32)
+
+    def blocks(*shape):
+        return pltpu.VMEM(shape, jnp.bfloat16)
+
+    other = swap(previous, 1)
+
     *asks, plan = pl.pallas_call(
-        functools.partial(ask_kernel, first, second, planes),
+        functools.partial(ask_kernel, room, planes),
         out_shape=[ints(width)] * steps + [ints((planes + 1) * width)],
-        in_specs=[SMEM] * 2,
+        in_specs=[HBM] * 2,
         out_specs=[SMEM] * (steps + 1),
-        scratch_shapes=[pltpu.SMEM((planes * width,), jnp.int32), pltpu.SMEM((2 * planes,), jnp.int32)],
+        scratch_shapes=[
+            pltpu.SMEM((slots,), jnp.int32),
+            pltpu.SMEM((slots,), jnp.int32),
+            pltpu.SMEM((planes * width,), jnp.int32),
+            pltpu.SMEM((2 * planes,), jnp.int32),
+            pltpu.SemaphoreType.DMA((2,)),
+        ],
         compiler_params=params(1),
-        cost_estimate=cost(0, 2000),
-    )(old_owner.reshape(slots), old_slot)
-    asked = [along(ask, -k) for k, ask in enumerate(asks, 1)]
-
-    near_block = lambda *shape: pltpu.VMEM(shape, jnp.bfloat16)
+        cost_estimate=cost(0, 1000),
+    )(far(old_owner.reshape(slots)), far(old_slot))
+    asked = [swap(ask, PLANE * k) for k, ask in enumerate(asks, 1)]
+
     cube, to_core, to_next, own = pl.pallas_call(
         prepare_kernel,
         out_shape=[
-            near_block(VOX, slots, channels),
-            near_block(LAYER, slots, channels),
-            near_block(LAYER, slots, channels),
-            near_block(*previous.shape),
-        ],
-        in_specs=[HBM] * 3 + [HBM],
+            blocks(VOX, slots, channels),
+            blocks(LAYER, slots, channels),
+            blocks(LAYER, slots, channels),
+            blocks(*previous.shape),
+        ],
+        in_specs=[HBM] * 5,
         out_specs=[VMEM] * 4,
         scratch_shapes=[
             pltpu.VMEM(features.shape, features.dtype),
@@ -343,28 +343,51 @@
             pltpu.SemaphoreType.DMA((3,)),
         ],
         compiler_params=params(4),
-        cost_estimate=cost(2 * EDGE * rows * (rows + VOX) * channels, 5 * rows * channels * 4),
-    )(far(features), far(occupancy), far(previous), plan)
-    from_core = beside(to_core, 1)
+        cost_estimate=cost(0, 1000),
+    )(far(features), far(occupancy), far(previous), plan, other)
+    from_core = swap(to_core, 1)
     from_next = lax.ppermute(
         to_next,
         "blk",
         [pair for i in range(1, count - 1, 2) for pair in ((i, i + 1), (i + 1, i))],
     )
 
-    early = pack(asked, [own, prev_c], 0, first)
-    sent = [along(part, k) for k, part in enumerate(early, 1)]
-    prev_yc = beside(lax.optimization_barrier((prev_y, early[0]))[0], 1)
-    pools = [own, prev_c, prev_y, prev_yc]
-    late = pack(asked, pools, first, second, [early[0], from_core, from_next])
-    sent += [along(part, k) for k, part in enumerate(late, 1)]
+    *parts, lists = pl.pallas_call(
+        functools.partial(same_kernel, room, steps),
+        out_shape=[blocks(room, VOX, channels)] * steps + [ints(planes * room)],
+        in_specs=[HBM] + [VMEM] * (2 + steps),
+        out_specs=[VMEM] * steps + [SMEM],
+        scratch_shapes=[
+            pltpu.SMEM((steps, width), jnp.int32),
+            pltpu.SMEM(plan.shape, jnp.int32),
+            pltpu.SemaphoreType.DMA((steps + 1,)),
+        ],
+        compiler_params=params(1),
+        cost_estimate=cost(0, 1000),
+    )(far(plan), *map(near, (own, other, *asked)))
+    early = [swap(part, PLANE * k) for k, part in enumerate(parts, 1)]
+    lists = swap(lists, 2)
+
+    parts = pl.pallas_call(
+        functools.partial(cross_kernel, room, planes),
+        out_shape=[blocks(room, VOX, channels)] * planes,
+        in_specs=[HBM] + [VMEM] * 2 + [HBM],
+        out_specs=[VMEM] * planes,
+        scratch_shapes=[pltpu.SMEM((planes * room,), jnp.int32), pltpu.SemaphoreType.DMA((1,))],
+        compiler_params=params(1),
+        cost_estimate=cost(0, 1000),
+    )(far(lists), near(own), near(other), from_next)
+    late = [swap(part, PLANE * k + 2) for k, part in enumerate(parts)]
 
     side = EDGE + 2
-    hidden = pl.pallas_call(
-        conv_kernel,
-        out_shape=pltpu.VMEM((slots, VOX, channels), jnp.float32),
-        in_specs=[VMEM] * 3 + [HBM] * 6,
-        out_specs=VMEM,
+    hidden, moved = pl.pallas_call(
+        functools.partial(conv_kernel, room, steps),
+        out_shape=[
+            pltpu.VMEM((slots, VOX, channels), jnp.float32),
+            blocks(slots + 1, VOX, channels),
+        ],
+        in_specs=[VMEM] * 5 + [HBM] * 7 + [VMEM] * steps,
+        out_specs=[VMEM] * 2,
         scratch_shapes=[
             pltpu.VMEM((side, side, side, slots, channels), jnp.bfloat16),
             pltpu.VMEM(conv_weight.shape, jnp.bfloat16),
@@ -373,37 +396,44 @@
             pltpu.VMEM(occupancy.shape, jnp.int32),
             pltpu.VMEM((1, channels), jnp.float32),
             pltpu.VMEM((1, channels), jnp.float32),
-            pltpu.SemaphoreType.DMA((7,)),
+            pltpu.SMEM(plan.shape, jnp.int32),
+            pltpu.SemaphoreType.DMA((8,)),
         ],
         compiler_params=params(12),
-        cost_estimate=cost(2 * 27 * EDGE * rows * channels * channels, 8000000),
+        cost_estimate=cost(0, 1000),
     )(
         near(cube),
         near(from_core),
         near(from_next),
+        *map(near, (own, other)),
         far(neighbors.T),
         far(occupancy),
         far(conv_weight),
         far(norm_scale[None]),
         far(norm_shift[None]),
-        late[0],
+        far(plan),
+        parts[0],
+        *map(near, early),
     )
 
     return pl.pallas_call(
-        functools.partial(finish_kernel, first, second, steps),
-        out_shape=jax.ShapeDtypeStruct((slots, VOX, channels), jnp.bfloat16),
-        in_specs=[HBM, VMEM, HBM] + [VMEM] * (PLANE + 2 * steps),
-        out_specs=HBM,
+        functools.partial(finish_kernel, room, planes),
+        out_shape=[
+            jax.ShapeDtypeStruct((slots, VOX, channels), jnp.bfloat16),
+            blocks(slots + 1, VOX, channels),
+        ],
+        in_specs=[HBM, VMEM, HBM, VMEM] + [VMEM] * planes,
+        out_specs=[HBM, VMEM],
+        input_output_aliases={3: 1},
         scratch_shapes=[
-            near_block(slots + 1, VOX, channels),
-            near_block(slots, VOX, channels),
-            pltpu.SMEM(((planes + 1) * width,), jnp.int32),
-            near_block(channels, channels),
+            blocks(slots, VOX, channels),
+            pltpu.SMEM(plan.shape, jnp.int32),
+            blocks(channels, channels),
             pltpu.SemaphoreType.DMA((2 + -(-slots // 4),)),
         ],
         compiler_params=params(4),
-        cost_estimate=cost(2 * VOX * slots * channels * channels, 3000000),
-    )(far(plan), near(hidden), far(prev_weight), *map(near, (*pools, *sent)))
+        cost_estimate=cost(0, 1000),
+    )(far(plan), near(hidden), far(prev_weight), near(moved), *map(near, late))[0]
 
 
 def solution(mesh):

time: 47.4 us -> 42.2 us (0.89); the launches traced: 47.2 us -> 41.4 us
  waiting for transfers between devices: 14 us -> 8.94 us
  local copies, waits for them, and re-layouts: 1.31 us -> 0.17 us
    ppermute x13, waiting for transfers between devices: 13.4 us -> 8.93 us  [swap(): return lax.ppermute(array, 'blk', [(i, i ^ flip) for i in range(count)])]
    unnamed x6 -> x4, local copies, waits for them, and re-layouts: 1.31 us -> 0.17 us
    ppermute x1, waiting for transfers between devices: 0.61 us -> 0.01 us  [per_device(): lax.ppermute(to_next, 'blk', [pair for i in range(1, count - 1, 2) for pa...]
    ppermute x13, starting transfers between devices: 15.1 us -> 15.7 us  [swap(): return lax.ppermute(array, 'blk', [(i, i ^ flip) for i in range(count)])]
    ppermute x1, starting transfers between devices: 3.53 us -> 3.05 us  [per_device(): lax.ppermute(to_next, 'blk', [pair for i in range(1, count - 1, 2) for pa...]
  transfers between devices with their start and end apart: 14 -> 14, of which waited for: 5 -> 3; matrix products, arithmetic and copies ran while one was open for 0% -> 0% of each run, Pallas kernels for 23% -> 28%
where the time goes in v2:
time: 42.2 us; the launch traced here: 41.4 us
  starting transfers between devices  18.7 us (44%)
  Pallas kernels  13.5 us (32%)
  waiting for transfers between devices  8.94 us (21%)
    ppermute x13, starting transfers between devices, swap(): return lax.ppermute(array, 'blk', [(i, i ^ flip) for i in range(count)])  15.7 us
    ppermute x13, waiting for transfers between devices, swap(): return lax.ppermute(array, 'blk', [(i, i ^ flip) for i in range(count)])  8.93 us
    pallas_call x1, Pallas kernels, per_device(): pl.pallas_call(functools.partial(conv_kernel, room, steps), out_shape=[pl...  6.1 us
    ppermute x1, starting transfers between devices, per_device(): lax.ppermute(to_next, 'blk', [pair for i in range(1, count - 1, 2) for pa...  3.05 us
    pallas_call x1, Pallas kernels, per_device(): pl.pallas_call(functools.partial(finish_kernel, room, planes), out_shape=...  1.99 us
    pallas_call x1, Pallas kernels, per_device(): pl.pallas_call(functools.partial(ask_kernel, room, planes), out_shape=[in...  1.64 us
    pallas_call x1, Pallas kernels, per_device(): pl.pallas_call(prepare_kernel, out_shape=[blocks(VOX, slots, channels), b...  1.51 us
    pallas_call x1, Pallas kernels, per_device(): pl.pallas_call(functools.partial(same_kernel, room, steps), out_shape=[bl...  1.38 us
  transfers between devices with their start and end apart: 14, of which 3 were waited for; matrix products, arithmetic and copies ran while one was open for 0% of the time, Pallas kernels for 28%

profile of v2, /device:TPU:11, one launch (start us, length us, event | category | flops | bytes accessed | tf_op | source)
XLA Modules:
  0.0 41.4 jit_solution(14792005679388364322)
XLA Ops:
  0.0 0.7 %collective-permute-start = (bf16[16,64,256]{2,1,0:T(8,128)(2,1)}, bf16[16,64,256]{2,1,0:T(8,128)(2,1)S(1)}, u32[]{:S(2)}, u32[]{:S(2)}) collective-permute-start(bf16[16,64,256]{2,1,0:T(8,128)(2,1)} %previous.1), channel_id=1, source_target_pairs={{0,1},{1,0},{2,3},{3,2},{4,5},{5,4},{6,7},{7,6},{8,9},{9,8},{10,11... | collective-permute-start | bytes 1572872 | tf_op jit(solution)/shard_map/ppermute | solution.py:303
  0.7 1.6 %shard_map.100 = (s32[8]{0:T(128)S(1)}, s32[8]{0:T(128)S(1)}, s32[8]{0:T(128)S(1)}, s32[40]{0:T(128)S(1)}) custom-call(s32[16]{0:T(128)} %bitcast.7, s32[16]{0:T(128)} %slot_in.1), custom_call_target="tpu_custom_call" | custom-call | bytes 1000 | tf_op jit(solution)/shard_map/pallas_call | solution.py:313
  2.3 0.0 copy-start
  2.3 0.2 collective-permute-start.3
  2.6 2.3 %collective-permute-start.4 = (s32[8]{0:T(128)S(1)}, s32[8]{0:T(128)S(1)}, u32[]{:S(2)}, u32[]{:S(2)}) collective-permute-start(s32[8]{0:T(128)S(1)} %get-tuple-element.30), channel_id=1, source_target_pairs={{0,8},{1,9},{2,10},{3,11},{4,12},{5,13},{6,14},{7,15},{8,0},{9,1},... | collective-permute-start | bytes 104 | tf_op jit(solution)/shard_map/ppermute | solution.py:303
  4.9 0.2 collective-permute-start.5
  5.0 0.0 collective-permute-done.after2.other
  5.1 1.5 %shard_map.101 = (bf16[64,16,256]{2,1,0:T(8,128)(2,1)S(1)}, bf16[16,16,256]{2,1,0:T(8,128)(2,1)S(1)}, bf16[16,16,256]{2,1,0:T(8,128)(2,1)S(1)}, bf16[16,64,256]{2,1,0:T(8,128)(2,1)S(1)}) custom-call(bf16[16,64,256]{2,1,0:T(8,128)(2,1)} %features.1, s32[16,64]{1,0:T(8,128)} %occupancy.3, bf16[16,64,256]{2,1,0:T(8,128)(2,1)} %previous.1, ...), custom_call_target="tpu_custom_call" | custom-call | bytes 1000 | tf_op jit(solution)/shard_map/pallas_call | solution.py:330
  6.6 0.9 %collective-permute-start.1 = (bf16[16,16,256]{2,1,0:T(8,128)(2,1)S(1)}, bf16[16,16,256]{2,1,0:T(8,128)(2,1)S(1)}, u32[]{:S(2)}, u32[]{:S(2)}) collective-permute-start(bf16[16,16,256]{2,1,0:T(8,128)(2,1)S(1)} %get-tuple-element.26), channel_id=1, source_target_pairs={{0,1},{1,0},{2,3},{3,2},{4,5},{5,4},{6,7},{7,6},{8,9},{9,8},{10,11... | collective-permute-start | bytes 393224 | tf_op jit(solution)/shard_map/ppermute | solution.py:303
  7.5 3.0 %collective-permute-start.2 = (bf16[16,16,256]{2,1,0:T(8,128)(2,1)S(1)}, bf16[16,16,256]{2,1,0:T(8,128)(2,1)S(1)}, u32[]{:S(2)}, u32[]{:S(2)}) collective-permute-start(bf16[16,16,256]{2,1,0:T(8,128)(2,1)S(1)} %get-tuple-element.27), channel_id=1, source_target_pairs={{1,2},{2,1},{3,4},{4,3},{5,6},{6,5},{7,8},{8,7},{9,10},{10,9},{11,... | collective-permute-start | bytes 393224 | tf_op jit(solution)/shard_map/ppermute | solution.py:349
  10.5 0.0 collective-permute-done.3.refs_0_
  10.5 0.0 collective-permute-done.4.refs_1_
  10.5 0.0 collective-permute-done.5.refs_2_
  10.6 0.0 copy-done
  10.6 1.4 %shard_map.102 = (bf16[4,64,256]{2,1,0:T(8,128)(2,1)S(1)}, bf16[4,64,256]{2,1,0:T(8,128)(2,1)S(1)}, bf16[4,64,256]{2,1,0:T(8,128)(2,1)S(1)}, s32[16]{0:T(128)S(1)}) custom-call(s32[40]{0:T(128)} %copy-done, bf16[16,64,256]{2,1,0:T(8,128)(2,1)S(1)} %get-tuple-element.28.own, bf16[16,64,256]{2,1,0:T(8,128)(2,1)S(1)} %collective-permute-done.after2.other, ...), custom_call_target="tpu_custom_call" | custom-call | bytes 1000 | tf_op jit(solution)/shard_map/pallas_call | solution.py:355
  12.0 1.1 %collective-permute-start.7 = (bf16[4,64,256]{2,1,0:T(8,128)(2,1)S(1)}, bf16[4,64,256]{2,1,0:T(8,128)(2,1)S(1)}, u32[]{:S(2)}, u32[]{:S(2)}) collective-permute-start(bf16[4,64,256]{2,1,0:T(8,128)(2,1)S(1)} %get-tuple-element.34), channel_id=1, source_target_pairs={{0,4},{1,5},{2,6},{3,7},{4,0},{5,1},{6,2},{7,3},{8,12},{9,13},{10,... | collective-permute-start | bytes 393224 | tf_op jit(solution)/shard_map/ppermute | solution.py:303
  13.1 2.2 %collective-permute-start.8 = (bf16[4,64,256]{2,1,0:T(8,128)(2,1)S(1)}, bf16[4,64,256]{2,1,0:T(8,128)(2,1)S(1)}, u32[]{:S(2)}, u32[]{:S(2)}) collective-permute-start(bf16[4,64,256]{2,1,0:T(8,128)(2,1)S(1)} %get-tuple-element.35), channel_id=1, source_target_pairs={{0,8},{1,9},{2,10},{3,11},{4,12},{5,13},{6,14},{7,15},{8,0},{9,1},... | collective-permute-start | bytes 393224 | tf_op jit(solution)/shard_map/ppermute | solution.py:303
  15.3 1.3 %collective-permute-start.6 = (s32[16]{0:T(128)S(1)}, s32[16]{0:T(128)S(1)}, u32[]{:S(2)}, u32[]{:S(2)}) collective-permute-start(s32[16]{0:T(128)S(1)} %get-tuple-element.32), channel_id=1, source_target_pairs={{0,2},{1,3},{2,0},{3,1},{4,6},{5,7},{6,4},{7,5},{8,10},{9,11},{10,... | collective-permute-start | bytes 200 | tf_op jit(solution)/shard_map/ppermute | solution.py:303
  16.6 1.2 %collective-permute-done.6.lists = s32[16]{0:T(128)S(1)} collective-permute-done((s32[16]{0:T(128)S(1)}, s32[16]{0:T(128)S(1)}, u32[]{:S(2)}, u32[]{:S(2)}) %collective-permute-start.6) | collective-permute-done | bytes 96 | tf_op jit(solution)/shard_map/ppermute | solution.py:303
  17.9 0.0 copy-start.1
  17.9 0.3 collective-permute-start.9
  18.2 0.0 collective-permute-done.2.after.next_
  18.2 0.2 copy-done.1
  18.4 0.9 %shard_map.103 = (bf16[4,64,256]{2,1,0:T(8,128)(2,1)S(1)}, bf16[4,64,256]{2,1,0:T(8,128)(2,1)S(1)}, bf16[4,64,256]{2,1,0:T(8,128)(2,1)S(1)}, bf16[4,64,256]{2,1,0:T(8,128)(2,1)S(1)}) custom-call(s32[16]{0:T(128)} %copy-done.1, bf16[16,64,256]{2,1,0:T(8,128)(2,1)S(1)} %get-tuple-element.28.own, bf16[16,64,256]{2,1,0:T(8,128)(2,1)S(1)} %collective-permute-done.after2.other, ...), custom_call_target="tpu_custom_call" | custom-call | bytes 1000 | tf_op jit(solution)/shard_map/pallas_call | solution.py:371
  19.3 1.9 %collective-permute-start.11 = (bf16[4,64,256]{2,1,0:T(8,128)(2,1)S(1)}, bf16[4,64,256]{2,1,0:T(8,128)(2,1)S(1)}, u32[]{:S(2)}, u32[]{:S(2)}) collective-permute-start(bf16[4,64,256]{2,1,0:T(8,128)(2,1)S(1)} %get-tuple-element.39), channel_id=1, source_target_pairs={{0,6},{1,7},{2,4},{3,5},{4,2},{5,3},{6,0},{7,1},{8,14},{9,15},{10,... | collective-permute-start | bytes 393224 | tf_op jit(solution)/shard_map/ppermute | solution.py:303
  21.2 0.0 collective-permute-done.1.core
  21.2 1.2 %collective-permute-start.12 = (bf16[4,64,256]{2,1,0:T(8,128)(2,1)S(1)}, bf16[4,64,256]{2,1,0:T(8,128)(2,1)S(1)}, u32[]{:S(2)}, u32[]{:S(2)}) collective-permute-start(bf16[4,64,256]{2,1,0:T(8,128)(2,1)S(1)} %get-tuple-element.40), channel_id=1, source_target_pairs={{0,10},{1,11},{2,8},{3,9},{4,14},{5,15},{6,12},{7,13},{8,2},{9,3},... | collective-permute-start | bytes 393224 | tf_op jit(solution)/shard_map/ppermute | solution.py:303
  22.4 0.0 collective-permute-done.7.refs_0_
  22.4 1.4 %collective-permute-start.13 = (bf16[4,64,256]{2,1,0:T(8,128)(2,1)S(1)}, bf16[4,64,256]{2,1,0:T(8,128)(2,1)S(1)}, u32[]{:S(2)}, u32[]{:S(2)}) collective-permute-start(bf16[4,64,256]{2,1,0:T(8,128)(2,1)S(1)} %get-tuple-element.41), channel_id=1, source_target_pairs={{0,14},{1,15},{2,12},{3,13},{4,10},{5,11},{6,8},{7,9},{8,6},{9,7},... | collective-permute-start | bytes 393224 | tf_op jit(solution)/shard_map/ppermute | solution.py:303
  23.8 0.0 collective-permute-done.8.refs_1_
  23.8 1.9 %collective-permute-start.10 = (bf16[4,64,256]{2,1,0:T(8,128)(2,1)S(1)}, bf16[4,64,256]{2,1,0:T(8,128)(2,1)S(1)}, u32[]{:S(2)}, u32[]{:S(2)}) collective-permute-start(bf16[4,64,256]{2,1,0:T(8,128)(2,1)S(1)} %get-tuple-element.33.after), channel_id=1, source_target_pairs={{0,2},{1,3},{2,0},{3,1},{4,6},{5,7},{6,4},{7,5},{8,10},{9,11},{10,... | collective-permute-start | bytes 393224 | tf_op jit(solution)/shard_map/ppermute | solution.py:303
  25.6 6.6 %collective-permute-done.9.refs_2_ = bf16[4,64,256]{2,1,0:T(8,128)(2,1)S(1)} collective-permute-done((bf16[4,64,256]{2,1,0:T(8,128)(2,1)S(1)}, bf16[4,64,256]{2,1,0:T(8,128)(2,1)S(1)}, u32[]{:S(2)}, u32[]{:S(2)}) %collective-permute-start.9) | collective-permute-done | bytes 131104 | tf_op jit(solution)/shard_map/ppermute | solution.py:303
  32.3 6.1 %shard_map.104 = (f32[16,64,256]{2,1,0:T(8,128)S(1)}, bf16[17,64,256]{2,1,0:T(8,128)(2,1)S(1)}) custom-call(bf16[64,16,256]{2,1,0:T(8,128)(2,1)S(1)} %get-tuple-element.25.cube, bf16[16,16,256]{2,1,0:T(8,128)(2,1)S(1)} %collective-permute-done.1.core, bf16[16,16,256]{2,1,0:T(8,128)(2,1)S(1)} %collective-permute-done.2.after.next_, ...), custom_call_target="tpu_custom_call" | custom-call | bytes 1000 | tf_op jit(solution)/shard_map/pallas_call | solution.py:383
  38.4 0.0 collective-permute-done.11.refs_1_
  38.4 0.0 collective-permute-done.12.refs_2_
  38.4 1.1 %collective-permute-done.13.refs_3_ = bf16[4,64,256]{2,1,0:T(8,128)(2,1)S(1)} collective-permute-done((bf16[4,64,256]{2,1,0:T(8,128)(2,1)S(1)}, bf16[4,64,256]{2,1,0:T(8,128)(2,1)S(1)}, u32[]{:S(2)}, u32[]{:S(2)}) %collective-permute-start.13) | collective-permute-done | bytes 131104 | tf_op jit(solution)/shard_map/ppermute | solution.py:303
  39.5 0.0 collective-permute-done.10.refs_0_
  39.5 2.0 %shard_map.105 = (bf16[16,64,256]{2,1,0:T(8,128)(2,1)}, bf16[17,64,256]{2,1,0:T(8,128)(2,1)S(1)}) custom-call(s32[40]{0:T(128)} %copy-done, f32[16,64,256]{2,1,0:T(8,128)S(1)} %get-tuple-element.37.hidden, bf16[256,256]{1,0:T(8,128)(2,1)} %weight.3, bf16[17,64,256]{2,1,0:T(8,128)(2,1)S(1)} %get-tuple-element.38.gathered, ...), custom_call_target="tpu_custom_call", output_to_operand_aliasing={{1}: (3, {})} | custom-call | bytes 1000 | tf_op jit(solution)/shard_map/pallas_call | solution.py:419
Async XLA Ops:
  0.0 5.0 %collective-permute-start = (bf16[16,64,256]{2,1,0:T(8,128)(2,1)}, bf16[16,64,256]{2,1,0:T(8,128)(2,1)S(1)}, u32[]{:S(2)}, u32[]{:S(2)}) collective-permute-start(bf16[16,64,256]{2,1,0:T(8,128)(2,1)} %previous.1), channel_id=1, source_target_pairs={{0,1},{1,0},{2,3},{3,2},{4,5},{5,4},{6,7},{7,6},{8,9},{9,8},{10,11... | collective-permute-start | bytes 1572872 | tf_op jit(solution)/shard_map/ppermute | solution.py:303
  2.3 8.2 %copy-start = (s32[40]{0:T(128)}, s32[40]{0:T(128)S(1)}, u32[]{:S(2)}) copy-start(s32[40]{0:T(128)S(1)} %get-tuple-element.24.after.plan) | copy-start | bytes 484
  2.3 8.2 %collective-permute-start.3 = (s32[8]{0:T(128)S(1)}, s32[8]{0:T(128)S(1)}, u32[]{:S(2)}, u32[]{:S(2)}) collective-permute-start(s32[8]{0:T(128)S(1)} %get-tuple-element.29), channel_id=1, source_target_pairs={{0,4},{1,5},{2,6},{3,7},{4,0},{5,1},{6,2},{7,3},{8,12},{9,13},{10,... | collective-permute-start | bytes 104 | tf_op jit(solution)/shard_map/ppermute | solution.py:303
  2.6 8.0 %collective-permute-start.4 = (s32[8]{0:T(128)S(1)}, s32[8]{0:T(128)S(1)}, u32[]{:S(2)}, u32[]{:S(2)}) collective-permute-start(s32[8]{0:T(128)S(1)} %get-tuple-element.30), channel_id=1, source_target_pairs={{0,8},{1,9},{2,10},{3,11},{4,12},{5,13},{6,14},{7,15},{8,0},{9,1},... | collective-permute-start | bytes 104 | tf_op jit(solution)/shard_map/ppermute | solution.py:303
  4.9 5.7 %collective-permute-start.5 = (s32[8]{0:T(128)S(1)}, s32[8]{0:T(128)S(1)}, u32[]{:S(2)}, u32[]{:S(2)}) collective-permute-start(s32[8]{0:T(128)S(1)} %get-tuple-element.31), channel_id=1, source_target_pairs={{0,12},{1,13},{2,14},{3,15},{4,8},{5,9},{6,10},{7,11},{8,4},{9,5},... | collective-permute-start | bytes 104 | tf_op jit(solution)/shard_map/ppermute | solution.py:303
  6.6 14.6 %collective-permute-start.1 = (bf16[16,16,256]{2,1,0:T(8,128)(2,1)S(1)}, bf16[16,16,256]{2,1,0:T(8,128)(2,1)S(1)}, u32[]{:S(2)}, u32[]{:S(2)}) collective-permute-start(bf16[16,16,256]{2,1,0:T(8,128)(2,1)S(1)} %get-tuple-element.26), channel_id=1, source_target_pairs={{0,1},{1,0},{2,3},{3,2},{4,5},{5,4},{6,7},{7,6},{8,9},{9,8},{10,11... | collective-permute-start | bytes 393224 | tf_op jit(solution)/shard_map/ppermute | solution.py:303
  7.5 10.7 %collective-permute-start.2 = (bf16[16,16,256]{2,1,0:T(8,128)(2,1)S(1)}, bf16[16,16,256]{2,1,0:T(8,128)(2,1)S(1)}, u32[]{:S(2)}, u32[]{:S(2)}) collective-permute-start(bf16[16,16,256]{2,1,0:T(8,128)(2,1)S(1)} %get-tuple-element.27), channel_id=1, source_target_pairs={{1,2},{2,1},{3,4},{4,3},{5,6},{6,5},{7,8},{8,7},{9,10},{10,9},{11,... | collective-permute-start | bytes 393224 | tf_op jit(solution)/shard_map/ppermute | solution.py:349
  12.0 10.4 %collective-permute-start.7 = (bf16[4,64,256]{2,1,0:T(8,128)(2,1)S(1)}, bf16[4,64,256]{2,1,0:T(8,128)(2,1)S(1)}, u32[]{:S(2)}, u32[]{:S(2)}) collective-permute-start(bf16[4,64,256]{2,1,0:T(8,128)(2,1)S(1)} %get-tuple-element.34), channel_id=1, source_target_pairs={{0,4},{1,5},{2,6},{3,7},{4,0},{5,1},{6,2},{7,3},{8,12},{9,13},{10,... | collective-permute-start | bytes 393224 | tf_op jit(solution)/shard_map/ppermute | solution.py:303
  13.1 10.7 %collective-permute-start.8 = (bf16[4,64,256]{2,1,0:T(8,128)(2,1)S(1)}, bf16[4,64,256]{2,1,0:T(8,128)(2,1)S(1)}, u32[]{:S(2)}, u32[]{:S(2)}) collective-permute-start(bf16[4,64,256]{2,1,0:T(8,128)(2,1)S(1)} %get-tuple-element.35), channel_id=1, source_target_pairs={{0,8},{1,9},{2,10},{3,11},{4,12},{5,13},{6,14},{7,15},{8,0},{9,1},... | collective-permute-start | bytes 393224 | tf_op jit(solution)/shard_map/ppermute | solution.py:303
  15.3 2.6 %collective-permute-start.6 = (s32[16]{0:T(128)S(1)}, s32[16]{0:T(128)S(1)}, u32[]{:S(2)}, u32[]{:S(2)}) collective-permute-start(s32[16]{0:T(128)S(1)} %get-tuple-element.32), channel_id=1, source_target_pairs={{0,2},{1,3},{2,0},{3,1},{4,6},{5,7},{6,4},{7,5},{8,10},{9,11},{10,... | collective-permute-start | bytes 200 | tf_op jit(solution)/shard_map/ppermute | solution.py:303
  17.9 0.5 %copy-start.1 = (s32[16]{0:T(128)}, s32[16]{0:T(128)S(1)}, u32[]{:S(2)}) copy-start(s32[16]{0:T(128)S(1)} %collective-permute-done.6.lists) | copy-start | bytes 196
  17.9 14.4 %collective-permute-start.9 = (bf16[4,64,256]{2,1,0:T(8,128)(2,1)S(1)}, bf16[4,64,256]{2,1,0:T(8,128)(2,1)S(1)}, u32[]{:S(2)}, u32[]{:S(2)}) collective-permute-start(bf16[4,64,256]{2,1,0:T(8,128)(2,1)S(1)} %get-tuple-element.36), channel_id=1, source_target_pairs={{0,12},{1,13},{2,14},{3,15},{4,8},{5,9},{6,10},{7,11},{8,4},{9,5},... | collective-permute-start | bytes 393224 | tf_op jit(solution)/shard_map/ppermute | solution.py:303
  19.3 19.1 %collective-permute-start.11 = (bf16[4,64,256]{2,1,0:T(8,128)(2,1)S(1)}, bf16[4,64,256]{2,1,0:T(8,128)(2,1)S(1)}, u32[]{:S(2)}, u32[]{:S(2)}) collective-permute-start(bf16[4,64,256]{2,1,0:T(8,128)(2,1)S(1)} %get-tuple-element.39), channel_id=1, source_target_pairs={{0,6},{1,7},{2,4},{3,5},{4,2},{5,3},{6,0},{7,1},{8,14},{9,15},{10,... | collective-permute-start | bytes 393224 | tf_op jit(solution)/shard_map/ppermute | solution.py:303
  21.2 17.2 %collective-permute-start.12 = (bf16[4,64,256]{2,1,0:T(8,128)(2,1)S(1)}, bf16[4,64,256]{2,1,0:T(8,128)(2,1)S(1)}, u32[]{:S(2)}, u32[]{:S(2)}) collective-permute-start(bf16[4,64,256]{2,1,0:T(8,128)(2,1)S(1)} %get-tuple-element.40), channel_id=1, source_target_pairs={{0,10},{1,11},{2,8},{3,9},{4,14},{5,15},{6,12},{7,13},{8,2},{9,3},... | collective-permute-start | bytes 393224 | tf_op jit(solution)/shard_map/ppermute | solution.py:303
  22.4 17.1 %collective-permute-start.13 = (bf16[4,64,256]{2,1,0:T(8,128)(2,1)S(1)}, bf16[4,64,256]{2,1,0:T(8,128)(2,1)S(1)}, u32[]{:S(2)}, u32[]{:S(2)}) collective-permute-start(bf16[4,64,256]{2,1,0:T(8,128)(2,1)S(1)} %get-tuple-element.41), channel_id=1, source_target_pairs={{0,14},{1,15},{2,12},{3,13},{4,10},{5,11},{6,8},{7,9},{8,6},{9,7},... | collective-permute-start | bytes 393224 | tf_op jit(solution)/shard_map/ppermute | solution.py:303
  23.8 15.7 %collective-permute-start.10 = (bf16[4,64,256]{2,1,0:T(8,128)(2,1)S(1)}, bf16[4,64,256]{2,1,0:T(8,128)(2,1)S(1)}, u32[]{:S(2)}, u32[]{:S(2)}) collective-permute-start(bf16[4,64,256]{2,1,0:T(8,128)(2,1)S(1)} %get-tuple-element.33.after), channel_id=1, source_target_pairs={{0,2},{1,3},{2,0},{3,1},{4,6},{5,7},{6,4},{7,5},{8,10},{9,11},{10,... | collective-permute-start | bytes 393224 | tf_op jit(solution)/shard_map/ppermute | solution.py:303

commit v3 on v2

--- a/solution.py
+++ b/solution.py
@@ -52,11 +52,12 @@
 
 
 def prepare_kernel(
-    features, occupancy, previous, after, after2, cube, core, next_, own, values_in, occ_in, sems
+    features, occupancy, previous, prev_weight, after, after2,
+    cube, core, next_, own, prev_taps, values_in, occ_in, sems,
 ):
     slots, _, channels = features.shape
     rows = LAYER * slots
-    copies = start_all(((features, values_in), (occupancy, occ_in), (previous, own)), sems)
+    copies = start_all(((features, values_in), (occupancy, occ_in), (previous, own), (prev_weight, prev_taps)), sems)
     row = lax.broadcasted_iota(jnp.int32, (rows, rows), 0)
     column = lax.broadcasted_iota(jnp.int32, (rows, rows), 1)
     swap = (row // slots == column % LAYER) & (row % slots == column // LAYER)
@@ -84,6 +85,7 @@
         next_[...] = cube[last]
 
     copies[2].wait()
+    copies[3].wait()
 
 
 def conv_kernel(
@@ -253,16 +255,15 @@
             fill(outs[k].at[i], own, other, lists_in[k * room + i])
 
 
-def finish_kernel(room, planes, plan, hidden, weight, gathered, *refs):
+def finish_kernel(room, planes, plan, hidden, weight_in, gathered, *refs):
     cross = refs[:planes]
-    out, moved, merged, plan_in, weight_in, sems = refs[planes:]
+    out, moved, merged, plan_in, sems = refs[planes:]
     slots = out.shape[0]
-    copies = start_all(((plan, plan_in), (weight, weight_in)), sems)
+    copies = start_all(((plan, plan_in),), sems)
     copies[0].wait()
     for k in range(planes):
         for i in range(room):
             moved[plan_in[(2 * k + 1) * room + i]] = cross[k][i]
-    copies[1].wait()
     group = min(4, slots)
     sent = []
     for j, g in enumerate(range(0, slots, group)):
@@ -273,7 +274,7 @@
         base = hidden[span].reshape(group * VOX, hidden.shape[2])
         done = jnp.where(base < 0.0, 0.0, base + projected)
         merged[span] = done.astype(out.dtype).reshape(group, VOX, out.shape[2])
-        sent.append(pltpu.make_async_copy(merged.at[span], out.at[span], sems.at[2 + j]))
+        sent.append(pltpu.make_async_copy(merged.at[span], out.at[span], sems.at[1 + j]))
         sent[-1].start()
     for copy in sent:
         copy.wait()
@@ -327,24 +328,25 @@
     )(far(old_owner.reshape(slots)), far(old_slot))
     asked = [swap(ask, PLANE * k) for k, ask in enumerate(asks, 1)]
 
-    cube, to_core, to_next, own = pl.pallas_call(
+    cube, to_core, to_next, own, prev_taps = pl.pallas_call(
         prepare_kernel,
         out_shape=[
             blocks(VOX, slots, channels),
             blocks(LAYER, slots, channels),
             blocks(LAYER, slots, channels),
             blocks(*previous.shape),
-        ],
-        in_specs=[HBM] * 5,
-        out_specs=[VMEM] * 4,
+            blocks(*prev_weight.shape),
+        ],
+        in_specs=[HBM] * 6,
+        out_specs=[VMEM] * 5,
         scratch_shapes=[
             pltpu.VMEM(features.shape, features.dtype),
             pltpu.VMEM(occupancy.shape, occupancy.dtype),
-            pltpu.SemaphoreType.DMA((3,)),
+            pltpu.SemaphoreType.DMA((4,)),
         ],
         compiler_params=params(4),
         cost_estimate=cost(0, 1000),
-    )(far(features), far(occupancy), far(previous), plan, other)
+    )(far(features), far(occupancy), far(previous), far(prev_weight), plan, other)
     from_core = swap(to_core, 1)
     from_next = lax.ppermute(
         to_next,
@@ -365,7 +367,8 @@
         compiler_params=params(1),
         cost_estimate=cost(0, 1000),
     )(far(plan), *map(near, (own, other, *asked)))
-    early = [swap(part, PLANE * k) for k, part in enumerate(parts, 1)]
+    early = {k: swap(parts[k - 1], PLANE * k) for k in sorted(range(1, planes), key=lambda k: k < 2)}
+    early = [early[k] for k in range(1, planes)]
     lists = swap(lists, 2)
 
     parts = pl.pallas_call(
@@ -377,7 +380,8 @@
         compiler_params=params(1),
         cost_estimate=cost(0, 1000),
     )(far(lists), near(own), near(other), from_next)
-    late = [swap(part, PLANE * k + 2) for k, part in enumerate(parts)]
+    late = {k: swap(parts[k], PLANE * k + 2) for k in sorted(range(planes), key=lambda k: k < 2)}
+    late = [late[k] for k in range(planes)]
 
     side = EDGE + 2
     hidden, moved = pl.pallas_call(
@@ -422,18 +426,17 @@
             jax.ShapeDtypeStruct((slots, VOX, channels), jnp.bfloat16),
             blocks(slots + 1, VOX, channels),
         ],
-        in_specs=[HBM, VMEM, HBM, VMEM] + [VMEM] * planes,
+        in_specs=[HBM, VMEM, VMEM, VMEM] + [VMEM] * planes,
         out_specs=[HBM, VMEM],
         input_output_aliases={3: 1},
         scratch_shapes=[
             blocks(slots, VOX, channels),
             pltpu.SMEM(plan.shape, jnp.int32),
-            blocks(channels, channels),
-            pltpu.SemaphoreType.DMA((2 + -(-slots // 4),)),
+            pltpu.SemaphoreType.DMA((1 + -(-slots // 4),)),
         ],
         compiler_params=params(4),
         cost_estimate=cost(0, 1000),
-    )(far(plan), near(hidden), far(prev_weight), near(moved), *map(near, late))[0]
+    )(far(plan), *map(near, (hidden, prev_taps, moved, *late)))[0]
 
 
 def solution(mesh):

time: 42.2 us -> 41.9 us (level)
  no operation moved by 1% of the time
where the time goes in v3:
time: 41.9 us; the launch traced here: 41.2 us
  starting transfers between devices  18.7 us (45%)
  Pallas kernels  13.3 us (32%)
  waiting for transfers between devices  8.93 us (21%)
    ppermute x13, starting transfers between devices, swap(): return lax.ppermute(array, 'blk', [(i, i ^ flip) for i in range(count)])  15.7 us
    ppermute x13, waiting for transfers between devices, swap(): return lax.ppermute(array, 'blk', [(i, i ^ flip) for i in range(count)])  8.93 us
    pallas_call x1, Pallas kernels, per_device(): pl.pallas_call(functools.partial(conv_kernel, room, steps), out_shape=[pl...  6.1 us
    ppermute x1, starting transfers between devices, per_device(): lax.ppermute(to_next, 'blk', [pair for i in range(1, count - 1, 2) for pa...  3.05 us
    pallas_call x1, Pallas kernels, per_device(): pl.pallas_call(functools.partial(finish_kernel, room, planes), out_shape=...  1.75 us
    pallas_call x1, Pallas kernels, per_device(): pl.pallas_call(functools.partial(ask_kernel, room, planes), out_shape=[in...  1.64 us
    pallas_call x1, Pallas kernels, per_device(): pl.pallas_call(prepare_kernel, out_shape=[blocks(VOX, slots, channels), b...  1.52 us
    pallas_call x1, Pallas kernels, per_device(): pl.pallas_call(functools.partial(same_kernel, room, steps), out_shape=[bl...  1.38 us
  transfers between devices with their start and end apart: 14, of which 3 were waited for; matrix products, arithmetic and copies ran while one was open for 0% of the time, Pallas kernels for 28%

profile of v3, /device:TPU:11, one launch (start us, length us, event | category | flops | bytes accessed | tf_op | source)
XLA Modules:
  0.0 41.2 jit_solution(2146015452488155829)
XLA Ops:
  0.0 0.7 %collective-permute-start = (bf16[16,64,256]{2,1,0:T(8,128)(2,1)}, bf16[16,64,256]{2,1,0:T(8,128)(2,1)S(1)}, u32[]{:S(2)}, u32[]{:S(2)}) collective-permute-start(bf16[16,64,256]{2,1,0:T(8,128)(2,1)} %previous.1), channel_id=1, source_target_pairs={{0,1},{1,0},{2,3},{3,2},{4,5},{5,4},{6,7},{7,6},{8,9},{9,8},{10,11... | collective-permute-start | bytes 1572872 | tf_op jit(solution)/shard_map/ppermute | solution.py:304
  0.7 1.6 %shard_map.100 = (s32[8]{0:T(128)S(1)}, s32[8]{0:T(128)S(1)}, s32[8]{0:T(128)S(1)}, s32[40]{0:T(128)S(1)}) custom-call(s32[16]{0:T(128)} %bitcast.7, s32[16]{0:T(128)} %slot_in.1), custom_call_target="tpu_custom_call" | custom-call | bytes 1000 | tf_op jit(solution)/shard_map/pallas_call | solution.py:314
  2.3 0.0 copy-start
  2.3 0.2 collective-permute-start.3
  2.6 2.3 %collective-permute-start.4 = (s32[8]{0:T(128)S(1)}, s32[8]{0:T(128)S(1)}, u32[]{:S(2)}, u32[]{:S(2)}) collective-permute-start(s32[8]{0:T(128)S(1)} %get-tuple-element.31), channel_id=1, source_target_pairs={{0,8},{1,9},{2,10},{3,11},{4,12},{5,13},{6,14},{7,15},{8,0},{9,1},... | collective-permute-start | bytes 104 | tf_op jit(solution)/shard_map/ppermute | solution.py:304
  4.9 0.2 collective-permute-start.5
  5.0 0.0 collective-permute-done.after2.other
  5.1 1.5 %shard_map.101 = (bf16[64,16,256]{2,1,0:T(8,128)(2,1)S(1)}, bf16[16,16,256]{2,1,0:T(8,128)(2,1)S(1)}, bf16[16,16,256]{2,1,0:T(8,128)(2,1)S(1)}, bf16[16,64,256]{2,1,0:T(8,128)(2,1)S(1)}, bf16[256,256]{1,0:T(8,128)(2,1)S(1)}) custom-call(bf16[16,64,256]{2,1,0:T(8,128)(2,1)} %features.1, s32[16,64]{1,0:T(8,128)} %occupancy.3, bf16[16,64,256]{2,1,0:T(8,128)(2,1)} %previous.1, ...), custom_call_target="tpu_custom_call" | custom-call | bytes 1000 | tf_op jit(solution)/shard_map/pallas_call | solution.py:331
  6.6 0.9 %collective-permute-start.1 = (bf16[16,16,256]{2,1,0:T(8,128)(2,1)S(1)}, bf16[16,16,256]{2,1,0:T(8,128)(2,1)S(1)}, u32[]{:S(2)}, u32[]{:S(2)}) collective-permute-start(bf16[16,16,256]{2,1,0:T(8,128)(2,1)S(1)} %get-tuple-element.27), channel_id=1, source_target_pairs={{0,1},{1,0},{2,3},{3,2},{4,5},{5,4},{6,7},{7,6},{8,9},{9,8},{10,11... | collective-permute-start | bytes 393224 | tf_op jit(solution)/shard_map/ppermute | solution.py:304
  7.5 3.0 %collective-permute-start.2 = (bf16[16,16,256]{2,1,0:T(8,128)(2,1)S(1)}, bf16[16,16,256]{2,1,0:T(8,128)(2,1)S(1)}, u32[]{:S(2)}, u32[]{:S(2)}) collective-permute-start(bf16[16,16,256]{2,1,0:T(8,128)(2,1)S(1)} %get-tuple-element.28), channel_id=1, source_target_pairs={{1,2},{2,1},{3,4},{4,3},{5,6},{6,5},{7,8},{8,7},{9,10},{10,9},{11,... | collective-permute-start | bytes 393224 | tf_op jit(solution)/shard_map/ppermute | solution.py:351
  10.5 0.0 collective-permute-done.3.refs_0_
  10.5 0.0 collective-permute-done.4.refs_1_
  10.6 0.0 collective-permute-done.5.refs_2_
  10.6 0.0 copy-done
  10.6 1.4 %shard_map.102 = (bf16[4,64,256]{2,1,0:T(8,128)(2,1)S(1)}, bf16[4,64,256]{2,1,0:T(8,128)(2,1)S(1)}, bf16[4,64,256]{2,1,0:T(8,128)(2,1)S(1)}, s32[16]{0:T(128)S(1)}) custom-call(s32[40]{0:T(128)} %copy-done, bf16[16,64,256]{2,1,0:T(8,128)(2,1)S(1)} %get-tuple-element.29.own, bf16[16,64,256]{2,1,0:T(8,128)(2,1)S(1)} %collective-permute-done.after2.other, ...), custom_call_target="tpu_custom_call" | custom-call | bytes 1000 | tf_op jit(solution)/shard_map/pallas_call | solution.py:357
  12.0 1.1 %collective-permute-start.7 = (bf16[4,64,256]{2,1,0:T(8,128)(2,1)S(1)}, bf16[4,64,256]{2,1,0:T(8,128)(2,1)S(1)}, u32[]{:S(2)}, u32[]{:S(2)}) collective-permute-start(bf16[4,64,256]{2,1,0:T(8,128)(2,1)S(1)} %get-tuple-element.35), channel_id=1, source_target_pairs={{0,4},{1,5},{2,6},{3,7},{4,0},{5,1},{6,2},{7,3},{8,12},{9,13},{10,... | collective-permute-start | bytes 393224 | tf_op jit(solution)/shard_map/ppermute | solution.py:304
  13.1 2.2 %collective-permute-start.8 = (bf16[4,64,256]{2,1,0:T(8,128)(2,1)S(1)}, bf16[4,64,256]{2,1,0:T(8,128)(2,1)S(1)}, u32[]{:S(2)}, u32[]{:S(2)}) collective-permute-start(bf16[4,64,256]{2,1,0:T(8,128)(2,1)S(1)} %get-tuple-element.36), channel_id=1, source_target_pairs={{0,8},{1,9},{2,10},{3,11},{4,12},{5,13},{6,14},{7,15},{8,0},{9,1},... | collective-permute-start | bytes 393224 | tf_op jit(solution)/shard_map/ppermute | solution.py:304
  15.3 1.3 %collective-permute-start.6 = (s32[16]{0:T(128)S(1)}, s32[16]{0:T(128)S(1)}, u32[]{:S(2)}, u32[]{:S(2)}) collective-permute-start(s32[16]{0:T(128)S(1)} %get-tuple-element.33), channel_id=1, source_target_pairs={{0,2},{1,3},{2,0},{3,1},{4,6},{5,7},{6,4},{7,5},{8,10},{9,11},{10,... | collective-permute-start | bytes 200 | tf_op jit(solution)/shard_map/ppermute | solution.py:304
  16.6 1.2 %collective-permute-done.6.lists = s32[16]{0:T(128)S(1)} collective-permute-done((s32[16]{0:T(128)S(1)}, s32[16]{0:T(128)S(1)}, u32[]{:S(2)}, u32[]{:S(2)}) %collective-permute-start.6) | collective-permute-done | bytes 96 | tf_op jit(solution)/shard_map/ppermute | solution.py:304
  17.9 0.0 copy-start.1
  17.9 0.3 collective-permute-start.9
  18.2 0.0 collective-permute-done.2.after.next_
  18.2 0.2 copy-done.1
  18.4 0.9 %shard_map.103 = (bf16[4,64,256]{2,1,0:T(8,128)(2,1)S(1)}, bf16[4,64,256]{2,1,0:T(8,128)(2,1)S(1)}, bf16[4,64,256]{2,1,0:T(8,128)(2,1)S(1)}, bf16[4,64,256]{2,1,0:T(8,128)(2,1)S(1)}) custom-call(s32[16]{0:T(128)} %copy-done.1, bf16[16,64,256]{2,1,0:T(8,128)(2,1)S(1)} %get-tuple-element.29.own, bf16[16,64,256]{2,1,0:T(8,128)(2,1)S(1)} %collective-permute-done.after2.other, ...), custom_call_target="tpu_custom_call" | custom-call | bytes 1000 | tf_op jit(solution)/shard_map/pallas_call | solution.py:374
  19.3 1.9 %collective-permute-start.11 = (bf16[4,64,256]{2,1,0:T(8,128)(2,1)S(1)}, bf16[4,64,256]{2,1,0:T(8,128)(2,1)S(1)}, u32[]{:S(2)}, u32[]{:S(2)}) collective-permute-start(bf16[4,64,256]{2,1,0:T(8,128)(2,1)S(1)} %get-tuple-element.41), channel_id=1, source_target_pairs={{0,6},{1,7},{2,4},{3,5},{4,2},{5,3},{6,0},{7,1},{8,14},{9,15},{10,... | collective-permute-start | bytes 393224 | tf_op jit(solution)/shard_map/ppermute | solution.py:304
  21.2 0.0 collective-permute-done.1.core
  21.2 1.2 %collective-permute-start.12 = (bf16[4,64,256]{2,1,0:T(8,128)(2,1)S(1)}, bf16[4,64,256]{2,1,0:T(8,128)(2,1)S(1)}, u32[]{:S(2)}, u32[]{:S(2)}) collective-permute-start(bf16[4,64,256]{2,1,0:T(8,128)(2,1)S(1)} %get-tuple-element.42), channel_id=1, source_target_pairs={{0,10},{1,11},{2,8},{3,9},{4,14},{5,15},{6,12},{7,13},{8,2},{9,3},... | collective-permute-start | bytes 393224 | tf_op jit(solution)/shard_map/ppermute | solution.py:304
  22.4 0.0 collective-permute-done.7.refs_0_
  22.4 1.4 %collective-permute-start.13 = (bf16[4,64,256]{2,1,0:T(8,128)(2,1)S(1)}, bf16[4,64,256]{2,1,0:T(8,128)(2,1)S(1)}, u32[]{:S(2)}, u32[]{:S(2)}) collective-permute-start(bf16[4,64,256]{2,1,0:T(8,128)(2,1)S(1)} %get-tuple-element.43), channel_id=1, source_target_pairs={{0,14},{1,15},{2,12},{3,13},{4,10},{5,11},{6,8},{7,9},{8,6},{9,7},... | collective-permute-start | bytes 393224 | tf_op jit(solution)/shard_map/ppermute | solution.py:304
  23.8 0.0 collective-permute-done.8.refs_1_
  23.8 1.9 %collective-permute-start.10 = (bf16[4,64,256]{2,1,0:T(8,128)(2,1)S(1)}, bf16[4,64,256]{2,1,0:T(8,128)(2,1)S(1)}, u32[]{:S(2)}, u32[]{:S(2)}) collective-permute-start(bf16[4,64,256]{2,1,0:T(8,128)(2,1)S(1)} %get-tuple-element.34.after), channel_id=1, source_target_pairs={{0,2},{1,3},{2,0},{3,1},{4,6},{5,7},{6,4},{7,5},{8,10},{9,11},{10,... | collective-permute-start | bytes 393224 | tf_op jit(solution)/shard_map/ppermute | solution.py:304
  25.7 6.6 %collective-permute-done.9.refs_2_ = bf16[4,64,256]{2,1,0:T(8,128)(2,1)S(1)} collective-permute-done((bf16[4,64,256]{2,1,0:T(8,128)(2,1)S(1)}, bf16[4,64,256]{2,1,0:T(8,128)(2,1)S(1)}, u32[]{:S(2)}, u32[]{:S(2)}) %collective-permute-start.9) | collective-permute-done | bytes 131104 | tf_op jit(solution)/shard_map/ppermute | solution.py:304
  32.3 6.1 %shard_map.104 = (f32[16,64,256]{2,1,0:T(8,128)S(1)}, bf16[17,64,256]{2,1,0:T(8,128)(2,1)S(1)}) custom-call(bf16[64,16,256]{2,1,0:T(8,128)(2,1)S(1)} %get-tuple-element.26.cube, bf16[16,16,256]{2,1,0:T(8,128)(2,1)S(1)} %collective-permute-done.1.core, bf16[16,16,256]{2,1,0:T(8,128)(2,1)S(1)} %collective-permute-done.2.after.next_, ...), custom_call_target="tpu_custom_call" | custom-call | bytes 1000 | tf_op jit(solution)/shard_map/pallas_call | solution.py:387
  38.4 0.0 collective-permute-done.11.refs_1_
  38.4 0.0 collective-permute-done.12.refs_2_
  38.4 1.0 %collective-permute-done.13.refs_3_ = bf16[4,64,256]{2,1,0:T(8,128)(2,1)S(1)} collective-permute-done((bf16[4,64,256]{2,1,0:T(8,128)(2,1)S(1)}, bf16[4,64,256]{2,1,0:T(8,128)(2,1)S(1)}, u32[]{:S(2)}, u32[]{:S(2)}) %collective-permute-start.13) | collective-permute-done | bytes 131104 | tf_op jit(solution)/shard_map/ppermute | solution.py:304
  39.5 0.0 collective-permute-done.10.refs_0_
  39.5 1.7 %shard_map.105 = (bf16[16,64,256]{2,1,0:T(8,128)(2,1)}, bf16[17,64,256]{2,1,0:T(8,128)(2,1)S(1)}) custom-call(s32[40]{0:T(128)} %copy-done, f32[16,64,256]{2,1,0:T(8,128)S(1)} %get-tuple-element.38.hidden, bf16[256,256]{1,0:T(8,128)(2,1)S(1)} %get-tuple-element.39.weight_in, ...), custom_call_target="tpu_custom_call", output_to_operand_aliasing={{1}: (3, {})} | custom-call | bytes 1000 | tf_op jit(solution)/shard_map/pallas_call | solution.py:423
Async XLA Ops:
  0.0 5.0 %collective-permute-start = (bf16[16,64,256]{2,1,0:T(8,128)(2,1)}, bf16[16,64,256]{2,1,0:T(8,128)(2,1)S(1)}, u32[]{:S(2)}, u32[]{:S(2)}) collective-permute-start(bf16[16,64,256]{2,1,0:T(8,128)(2,1)} %previous.1), channel_id=1, source_target_pairs={{0,1},{1,0},{2,3},{3,2},{4,5},{5,4},{6,7},{7,6},{8,9},{9,8},{10,11... | collective-permute-start | bytes 1572872 | tf_op jit(solution)/shard_map/ppermute | solution.py:304
  2.3 8.2 %copy-start = (s32[40]{0:T(128)}, s32[40]{0:T(128)S(1)}, u32[]{:S(2)}) copy-start(s32[40]{0:T(128)S(1)} %get-tuple-element.25.after.plan) | copy-start | bytes 484
  2.3 8.2 %collective-permute-start.3 = (s32[8]{0:T(128)S(1)}, s32[8]{0:T(128)S(1)}, u32[]{:S(2)}, u32[]{:S(2)}) collective-permute-start(s32[8]{0:T(128)S(1)} %get-tuple-element.30), channel_id=1, source_target_pairs={{0,4},{1,5},{2,6},{3,7},{4,0},{5,1},{6,2},{7,3},{8,12},{9,13},{10,... | collective-permute-start | bytes 104 | tf_op jit(solution)/shard_map/ppermute | solution.py:304
  2.6 8.0 %collective-permute-start.4 = (s32[8]{0:T(128)S(1)}, s32[8]{0:T(128)S(1)}, u32[]{:S(2)}, u32[]{:S(2)}) collective-permute-start(s32[8]{0:T(128)S(1)} %get-tuple-element.31), channel_id=1, source_target_pairs={{0,8},{1,9},{2,10},{3,11},{4,12},{5,13},{6,14},{7,15},{8,0},{9,1},... | collective-permute-start | bytes 104 | tf_op jit(solution)/shard_map/ppermute | solution.py:304
  4.9 5.7 %collective-permute-start.5 = (s32[8]{0:T(128)S(1)}, s32[8]{0:T(128)S(1)}, u32[]{:S(2)}, u32[]{:S(2)}) collective-permute-start(s32[8]{0:T(128)S(1)} %get-tuple-element.32), channel_id=1, source_target_pairs={{0,12},{1,13},{2,14},{3,15},{4,8},{5,9},{6,10},{7,11},{8,4},{9,5},... | collective-permute-start | bytes 104 | tf_op jit(solution)/shard_map/ppermute | solution.py:304
  6.6 14.6 %collective-permute-start.1 = (bf16[16,16,256]{2,1,0:T(8,128)(2,1)S(1)}, bf16[16,16,256]{2,1,0:T(8,128)(2,1)S(1)}, u32[]{:S(2)}, u32[]{:S(2)}) collective-permute-start(bf16[16,16,256]{2,1,0:T(8,128)(2,1)S(1)} %get-tuple-element.27), channel_id=1, source_target_pairs={{0,1},{1,0},{2,3},{3,2},{4,5},{5,4},{6,7},{7,6},{8,9},{9,8},{10,11... | collective-permute-start | bytes 393224 | tf_op jit(solution)/shard_map/ppermute | solution.py:304
  7.5 10.7 %collective-permute-start.2 = (bf16[16,16,256]{2,1,0:T(8,128)(2,1)S(1)}, bf16[16,16,256]{2,1,0:T(8,128)(2,1)S(1)}, u32[]{:S(2)}, u32[]{:S(2)}) collective-permute-start(bf16[16,16,256]{2,1,0:T(8,128)(2,1)S(1)} %get-tuple-element.28), channel_id=1, source_target_pairs={{1,2},{2,1},{3,4},{4,3},{5,6},{6,5},{7,8},{8,7},{9,10},{10,9},{11,... | collective-permute-start | bytes 393224 | tf_op jit(solution)/shard_map/ppermute | solution.py:351
  12.0 10.4 %collective-permute-start.7 = (bf16[4,64,256]{2,1,0:T(8,128)(2,1)S(1)}, bf16[4,64,256]{2,1,0:T(8,128)(2,1)S(1)}, u32[]{:S(2)}, u32[]{:S(2)}) collective-permute-start(bf16[4,64,256]{2,1,0:T(8,128)(2,1)S(1)} %get-tuple-element.35), channel_id=1, source_target_pairs={{0,4},{1,5},{2,6},{3,7},{4,0},{5,1},{6,2},{7,3},{8,12},{9,13},{10,... | collective-permute-start | bytes 393224 | tf_op jit(solution)/shard_map/ppermute | solution.py:304
  13.1 10.7 %collective-permute-start.8 = (bf16[4,64,256]{2,1,0:T(8,128)(2,1)S(1)}, bf16[4,64,256]{2,1,0:T(8,128)(2,1)S(1)}, u32[]{:S(2)}, u32[]{:S(2)}) collective-permute-start(bf16[4,64,256]{2,1,0:T(8,128)(2,1)S(1)} %get-tuple-element.36), channel_id=1, source_target_pairs={{0,8},{1,9},{2,10},{3,11},{4,12},{5,13},{6,14},{7,15},{8,0},{9,1},... | collective-permute-start | bytes 393224 | tf_op jit(solution)/shard_map/ppermute | solution.py:304
  15.3 2.6 %collective-permute-start.6 = (s32[16]{0:T(128)S(1)}, s32[16]{0:T(128)S(1)}, u32[]{:S(2)}, u32[]{:S(2)}) collective-permute-start(s32[16]{0:T(128)S(1)} %get-tuple-element.33), channel_id=1, source_target_pairs={{0,2},{1,3},{2,0},{3,1},{4,6},{5,7},{6,4},{7,5},{8,10},{9,11},{10,... | collective-permute-start | bytes 200 | tf_op jit(solution)/shard_map/ppermute | solution.py:304
  17.9 0.5 %copy-start.1 = (s32[16]{0:T(128)}, s32[16]{0:T(128)S(1)}, u32[]{:S(2)}) copy-start(s32[16]{0:T(128)S(1)} %collective-permute-done.6.lists) | copy-start | bytes 196
  17.9 14.4 %collective-permute-start.9 = (bf16[4,64,256]{2,1,0:T(8,128)(2,1)S(1)}, bf16[4,64,256]{2,1,0:T(8,128)(2,1)S(1)}, u32[]{:S(2)}, u32[]{:S(2)}) collective-permute-start(bf16[4,64,256]{2,1,0:T(8,128)(2,1)S(1)} %get-tuple-element.37), channel_id=1, source_target_pairs={{0,12},{1,13},{2,14},{3,15},{4,8},{5,9},{6,10},{7,11},{8,4},{9,5},... | collective-permute-start | bytes 393224 | tf_op jit(solution)/shard_map/ppermute | solution.py:304
  19.3 19.1 %collective-permute-start.11 = (bf16[4,64,256]{2,1,0:T(8,128)(2,1)S(1)}, bf16[4,64,256]{2,1,0:T(8,128)(2,1)S(1)}, u32[]{:S(2)}, u32[]{:S(2)}) collective-permute-start(bf16[4,64,256]{2,1,0:T(8,128)(2,1)S(1)} %get-tuple-element.41), channel_id=1, source_target_pairs={{0,6},{1,7},{2,4},{3,5},{4,2},{5,3},{6,0},{7,1},{8,14},{9,15},{10,... | collective-permute-start | bytes 393224 | tf_op jit(solution)/shard_map/ppermute | solution.py:304
  21.2 17.2 %collective-permute-start.12 = (bf16[4,64,256]{2,1,0:T(8,128)(2,1)S(1)}, bf16[4,64,256]{2,1,0:T(8,128)(2,1)S(1)}, u32[]{:S(2)}, u32[]{:S(2)}) collective-permute-start(bf16[4,64,256]{2,1,0:T(8,128)(2,1)S(1)} %get-tuple-element.42), channel_id=1, source_target_pairs={{0,10},{1,11},{2,8},{3,9},{4,14},{5,15},{6,12},{7,13},{8,2},{9,3},... | collective-permute-start | bytes 393224 | tf_op jit(solution)/shard_map/ppermute | solution.py:304
  22.4 17.1 %collective-permute-start.13 = (bf16[4,64,256]{2,1,0:T(8,128)(2,1)S(1)}, bf16[4,64,256]{2,1,0:T(8,128)(2,1)S(1)}, u32[]{:S(2)}, u32[]{:S(2)}) collective-permute-start(bf16[4,64,256]{2,1,0:T(8,128)(2,1)S(1)} %get-tuple-element.43), channel_id=1, source_target_pairs={{0,14},{1,15},{2,12},{3,13},{4,10},{5,11},{6,8},{7,9},{8,6},{9,7},... | collective-permute-start | bytes 393224 | tf_op jit(solution)/shard_map/ppermute | solution.py:304
  23.8 15.7 %collective-permute-start.10 = (bf16[4,64,256]{2,1,0:T(8,128)(2,1)S(1)}, bf16[4,64,256]{2,1,0:T(8,128)(2,1)S(1)}, u32[]{:S(2)}, u32[]{:S(2)}) collective-permute-start(bf16[4,64,256]{2,1,0:T(8,128)(2,1)S(1)} %get-tuple-element.34.after), channel_id=1, source_target_pairs={{0,2},{1,3},{2,0},{3,1},{4,6},{5,7},{6,4},{7,5},{8,10},{9,11},{10,... | collective-permute-start | bytes 393224 | tf_op jit(solution)/shard_map/ppermute | solution.py:304

commit v4 on v3

--- a/solution.py
+++ b/solution.py
@@ -357,7 +357,7 @@
     *parts, lists = pl.pallas_call(
         functools.partial(same_kernel, room, steps),
         out_shape=[blocks(room, VOX, channels)] * steps + [ints(planes * room)],
-        in_specs=[HBM] + [VMEM] * (2 + steps),
+        in_specs=[VMEM] * (3 + steps),
         out_specs=[VMEM] * steps + [SMEM],
         scratch_shapes=[
             pltpu.SMEM((steps, width), jnp.int32),
@@ -366,7 +366,7 @@
         ],
         compiler_params=params(1),
         cost_estimate=cost(0, 1000),
-    )(far(plan), *map(near, (own, other, *asked)))
+    )(*map(near, (plan, own, other, *asked)))
     early = {k: swap(parts[k - 1], PLANE * k) for k in sorted(range(1, planes), key=lambda k: k < 2)}
     early = [early[k] for k in range(1, planes)]
     lists = swap(lists, 2)
@@ -374,12 +374,12 @@
     parts = pl.pallas_call(
         functools.partial(cross_kernel, room, planes),
         out_shape=[blocks(room, VOX, channels)] * planes,
-        in_specs=[HBM] + [VMEM] * 2 + [HBM],
+        in_specs=[VMEM] * 3 + [HBM],
         out_specs=[VMEM] * planes,
         scratch_shapes=[pltpu.SMEM((planes * room,), jnp.int32), pltpu.SemaphoreType.DMA((1,))],
         compiler_params=params(1),
         cost_estimate=cost(0, 1000),
-    )(far(lists), near(own), near(other), from_next)
+    )(near(lists), near(own), near(other), from_next)
     late = {k: swap(parts[k], PLANE * k + 2) for k in sorted(range(planes), key=lambda k: k < 2)}
     late = [late[k] for k in range(planes)]
 
@@ -390,7 +390,7 @@
             pltpu.VMEM((slots, VOX, channels), jnp.float32),
             blocks(slots + 1, VOX, channels),
         ],
-        in_specs=[VMEM] * 5 + [HBM] * 7 + [VMEM] * steps,
+        in_specs=[VMEM] * 5 + [HBM] * 5 + [VMEM, HBM] + [VMEM] * steps,
         out_specs=[VMEM] * 2,
         scratch_shapes=[
             pltpu.VMEM((side, side, side, slots, channels), jnp.bfloat16),
@@ -415,7 +415,7 @@
         far(conv_weight),
         far(norm_scale[None]),
         far(norm_shift[None]),
-        far(plan),
+        near(plan),
         parts[0],
         *map(near, early),
     )
@@ -426,7 +426,7 @@
             jax.ShapeDtypeStruct((slots, VOX, channels), jnp.bfloat16),
             blocks(slots + 1, VOX, channels),
         ],
-        in_specs=[HBM, VMEM, VMEM, VMEM] + [VMEM] * planes,
+        in_specs=[VMEM] * (4 + planes),
         out_specs=[HBM, VMEM],
         input_output_aliases={3: 1},
         scratch_shapes=[
@@ -436,7 +436,7 @@
         ],
         compiler_params=params(4),
         cost_estimate=cost(0, 1000),
-    )(far(plan), *map(near, (hidden, prev_taps, moved, *late)))[0]
+    )(*map(near, (plan, hidden, prev_taps, moved, *late)))[0]
 
 
 def solution(mesh):

time: 41.9 us -> 41.8 us (level)
  no operation moved by 1% of the time
where the time goes in v4:
time: 41.8 us; the launch traced here: 41.1 us
  starting transfers between devices  19.1 us (46%)
  Pallas kernels  13 us (31%)
  waiting for transfers between devices  8.88 us (21%)
    ppermute x13, starting transfers between devices, swap(): return lax.ppermute(array, 'blk', [(i, i ^ flip) for i in range(count)])  16.1 us
    ppermute x13, waiting for transfers between devices, swap(): return lax.ppermute(array, 'blk', [(i, i ^ flip) for i in range(count)])  8.88 us
    pallas_call x1, Pallas kernels, per_device(): pl.pallas_call(functools.partial(conv_kernel, room, steps), out_shape=[pl...  6.03 us
    ppermute x1, starting transfers between devices, per_device(): lax.ppermute(to_next, 'blk', [pair for i in range(1, count - 1, 2) for pa...  3.05 us
    pallas_call x1, Pallas kernels, per_device(): pl.pallas_call(functools.partial(ask_kernel, room, planes), out_shape=[in...  1.64 us
    pallas_call x1, Pallas kernels, per_device(): pl.pallas_call(functools.partial(finish_kernel, room, planes), out_shape=...  1.63 us
    pallas_call x1, Pallas kernels, per_device(): pl.pallas_call(prepare_kernel, out_shape=[blocks(VOX, slots, channels), b...  1.52 us
    pallas_call x1, Pallas kernels, per_device(): pl.pallas_call(functools.partial(same_kernel, room, steps), out_shape=[bl...  1.38 us
  transfers between devices with their start and end apart: 14, of which 3 were waited for; matrix products, arithmetic and copies ran while one was open for 0% of the time, Pallas kernels for 28%

profile of v4, /device:TPU:11, one launch (start us, length us, event | category | flops | bytes accessed | tf_op | source)
XLA Modules:
  0.0 41.1 jit_solution(15203681176329544859)
XLA Ops:
  0.0 0.7 %collective-permute-start = (bf16[16,64,256]{2,1,0:T(8,128)(2,1)}, bf16[16,64,256]{2,1,0:T(8,128)(2,1)S(1)}, u32[]{:S(2)}, u32[]{:S(2)}) collective-permute-start(bf16[16,64,256]{2,1,0:T(8,128)(2,1)} %previous.1), channel_id=1, source_target_pairs={{0,1},{1,0},{2,3},{3,2},{4,5},{5,4},{6,7},{7,6},{8,9},{9,8},{10,11... | collective-permute-start | bytes 1572872 | tf_op jit(solution)/shard_map/ppermute | solution.py:304
  0.7 1.6 %shard_map.100 = (s32[8]{0:T(128)S(1)}, s32[8]{0:T(128)S(1)}, s32[8]{0:T(128)S(1)}, s32[40]{0:T(128)S(1)}) custom-call(s32[16]{0:T(128)} %bitcast.7, s32[16]{0:T(128)} %slot_in.1), custom_call_target="tpu_custom_call" | custom-call | bytes 1000 | tf_op jit(solution)/shard_map/pallas_call | solution.py:314
  2.3 0.2 collective-permute-start.3
  2.6 2.3 %collective-permute-start.4 = (s32[8]{0:T(128)S(1)}, s32[8]{0:T(128)S(1)}, u32[]{:S(2)}, u32[]{:S(2)}) collective-permute-start(s32[8]{0:T(128)S(1)} %get-tuple-element.31), channel_id=1, source_target_pairs={{0,8},{1,9},{2,10},{3,11},{4,12},{5,13},{6,14},{7,15},{8,0},{9,1},... | collective-permute-start | bytes 104 | tf_op jit(solution)/shard_map/ppermute | solution.py:304
  4.9 0.2 collective-permute-start.5
  5.0 0.0 collective-permute-done.after2.other
  5.0 1.5 %shard_map.101 = (bf16[64,16,256]{2,1,0:T(8,128)(2,1)S(1)}, bf16[16,16,256]{2,1,0:T(8,128)(2,1)S(1)}, bf16[16,16,256]{2,1,0:T(8,128)(2,1)S(1)}, bf16[16,64,256]{2,1,0:T(8,128)(2,1)S(1)}, bf16[256,256]{1,0:T(8,128)(2,1)S(1)}) custom-call(bf16[16,64,256]{2,1,0:T(8,128)(2,1)} %features.1, s32[16,64]{1,0:T(8,128)} %occupancy.3, bf16[16,64,256]{2,1,0:T(8,128)(2,1)} %previous.1, ...), custom_call_target="tpu_custom_call" | custom-call | bytes 1000 | tf_op jit(solution)/shard_map/pallas_call | solution.py:331
  6.6 0.9 %collective-permute-start.1 = (bf16[16,16,256]{2,1,0:T(8,128)(2,1)S(1)}, bf16[16,16,256]{2,1,0:T(8,128)(2,1)S(1)}, u32[]{:S(2)}, u32[]{:S(2)}) collective-permute-start(bf16[16,16,256]{2,1,0:T(8,128)(2,1)S(1)} %get-tuple-element.27), channel_id=1, source_target_pairs={{0,1},{1,0},{2,3},{3,2},{4,5},{5,4},{6,7},{7,6},{8,9},{9,8},{10,11... | collective-permute-start | bytes 393224 | tf_op jit(solution)/shard_map/ppermute | solution.py:304
  7.5 3.0 %collective-permute-start.2 = (bf16[16,16,256]{2,1,0:T(8,128)(2,1)S(1)}, bf16[16,16,256]{2,1,0:T(8,128)(2,1)S(1)}, u32[]{:S(2)}, u32[]{:S(2)}) collective-permute-start(bf16[16,16,256]{2,1,0:T(8,128)(2,1)S(1)} %get-tuple-element.28), channel_id=1, source_target_pairs={{1,2},{2,1},{3,4},{4,3},{5,6},{6,5},{7,8},{8,7},{9,10},{10,9},{11,... | collective-permute-start | bytes 393224 | tf_op jit(solution)/shard_map/ppermute | solution.py:351
  10.5 0.0 collective-permute-done.3.refs_0_
  10.5 0.0 collective-permute-done.4.refs_1_
  10.6 0.0 collective-permute-done.5.refs_2_
  10.6 1.4 %shard_map.102 = (bf16[4,64,256]{2,1,0:T(8,128)(2,1)S(1)}, bf16[4,64,256]{2,1,0:T(8,128)(2,1)S(1)}, bf16[4,64,256]{2,1,0:T(8,128)(2,1)S(1)}, s32[16]{0:T(128)S(1)}) custom-call(s32[40]{0:T(128)S(1)} %get-tuple-element.25.after.plan, bf16[16,64,256]{2,1,0:T(8,128)(2,1)S(1)} %get-tuple-element.29.own, ...), custom_call_target="tpu_custom_call" | custom-call | bytes 1000 | tf_op jit(solution)/shard_map/pallas_call | solution.py:357
  11.9 1.1 %collective-permute-start.7 = (bf16[4,64,256]{2,1,0:T(8,128)(2,1)S(1)}, bf16[4,64,256]{2,1,0:T(8,128)(2,1)S(1)}, u32[]{:S(2)}, u32[]{:S(2)}) collective-permute-start(bf16[4,64,256]{2,1,0:T(8,128)(2,1)S(1)} %get-tuple-element.35), channel_id=1, source_target_pairs={{0,4},{1,5},{2,6},{3,7},{4,0},{5,1},{6,2},{7,3},{8,12},{9,13},{10,... | collective-permute-start | bytes 393224 | tf_op jit(solution)/shard_map/ppermute | solution.py:304
  13.1 2.2 %collective-permute-start.8 = (bf16[4,64,256]{2,1,0:T(8,128)(2,1)S(1)}, bf16[4,64,256]{2,1,0:T(8,128)(2,1)S(1)}, u32[]{:S(2)}, u32[]{:S(2)}) collective-permute-start(bf16[4,64,256]{2,1,0:T(8,128)(2,1)S(1)} %get-tuple-element.36), channel_id=1, source_target_pairs={{0,8},{1,9},{2,10},{3,11},{4,12},{5,13},{6,14},{7,15},{8,0},{9,1},... | collective-permute-start | bytes 393224 | tf_op jit(solution)/shard_map/ppermute | solution.py:304
  15.3 1.3 %collective-permute-start.6 = (s32[16]{0:T(128)S(1)}, s32[16]{0:T(128)S(1)}, u32[]{:S(2)}, u32[]{:S(2)}) collective-permute-start(s32[16]{0:T(128)S(1)} %get-tuple-element.33), channel_id=1, source_target_pairs={{0,2},{1,3},{2,0},{3,1},{4,6},{5,7},{6,4},{7,5},{8,10},{9,11},{10,... | collective-permute-start | bytes 200 | tf_op jit(solution)/shard_map/ppermute | solution.py:304
  16.6 1.2 %collective-permute-done.6.lists = s32[16]{0:T(128)S(1)} collective-permute-done((s32[16]{0:T(128)S(1)}, s32[16]{0:T(128)S(1)}, u32[]{:S(2)}, u32[]{:S(2)}) %collective-permute-start.6) | collective-permute-done | bytes 96 | tf_op jit(solution)/shard_map/ppermute | solution.py:304
  17.9 0.3 collective-permute-start.9
  18.2 0.0 collective-permute-done.2.after.next_
  18.2 0.8 %shard_map.103 = (bf16[4,64,256]{2,1,0:T(8,128)(2,1)S(1)}, bf16[4,64,256]{2,1,0:T(8,128)(2,1)S(1)}, bf16[4,64,256]{2,1,0:T(8,128)(2,1)S(1)}, bf16[4,64,256]{2,1,0:T(8,128)(2,1)S(1)}) custom-call(s32[16]{0:T(128)S(1)} %collective-permute-done.6.lists, bf16[16,64,256]{2,1,0:T(8,128)(2,1)S(1)} %get-tuple-element.29.own, ...), custom_call_target="tpu_custom_call" | custom-call | bytes 1000 | tf_op jit(solution)/shard_map/pallas_call | solution.py:374
  19.0 2.1 %collective-permute-start.11 = (bf16[4,64,256]{2,1,0:T(8,128)(2,1)S(1)}, bf16[4,64,256]{2,1,0:T(8,128)(2,1)S(1)}, u32[]{:S(2)}, u32[]{:S(2)}) collective-permute-start(bf16[4,64,256]{2,1,0:T(8,128)(2,1)S(1)} %get-tuple-element.41), channel_id=1, source_target_pairs={{0,6},{1,7},{2,4},{3,5},{4,2},{5,3},{6,0},{7,1},{8,14},{9,15},{10,... | collective-permute-start | bytes 393224 | tf_op jit(solution)/shard_map/ppermute | solution.py:304
  21.1 0.0 collective-permute-done.1.core
  21.1 1.2 %collective-permute-start.12 = (bf16[4,64,256]{2,1,0:T(8,128)(2,1)S(1)}, bf16[4,64,256]{2,1,0:T(8,128)(2,1)S(1)}, u32[]{:S(2)}, u32[]{:S(2)}) collective-permute-start(bf16[4,64,256]{2,1,0:T(8,128)(2,1)S(1)} %get-tuple-element.42), channel_id=1, source_target_pairs={{0,10},{1,11},{2,8},{3,9},{4,14},{5,15},{6,12},{7,13},{8,2},{9,3},... | collective-permute-start | bytes 393224 | tf_op jit(solution)/shard_map/ppermute | solution.py:304
  22.2 0.0 collective-permute-done.7.refs_0_
  22.3 1.3 %collective-permute-start.13 = (bf16[4,64,256]{2,1,0:T(8,128)(2,1)S(1)}, bf16[4,64,256]{2,1,0:T(8,128)(2,1)S(1)}, u32[]{:S(2)}, u32[]{:S(2)}) collective-permute-start(bf16[4,64,256]{2,1,0:T(8,128)(2,1)S(1)} %get-tuple-element.43), channel_id=1, source_target_pairs={{0,14},{1,15},{2,12},{3,13},{4,10},{5,11},{6,8},{7,9},{8,6},{9,7},... | collective-permute-start | bytes 393224 | tf_op jit(solution)/shard_map/ppermute | solution.py:304
  23.6 0.0 collective-permute-done.8.refs_1_
  23.6 2.2 %collective-permute-start.10 = (bf16[4,64,256]{2,1,0:T(8,128)(2,1)S(1)}, bf16[4,64,256]{2,1,0:T(8,128)(2,1)S(1)}, u32[]{:S(2)}, u32[]{:S(2)}) collective-permute-start(bf16[4,64,256]{2,1,0:T(8,128)(2,1)S(1)} %get-tuple-element.34.after), channel_id=1, source_target_pairs={{0,2},{1,3},{2,0},{3,1},{4,6},{5,7},{6,4},{7,5},{8,10},{9,11},{10,... | collective-permute-start | bytes 393224 | tf_op jit(solution)/shard_map/ppermute | solution.py:304
  25.8 6.7 %collective-permute-done.9.refs_2_ = bf16[4,64,256]{2,1,0:T(8,128)(2,1)S(1)} collective-permute-done((bf16[4,64,256]{2,1,0:T(8,128)(2,1)S(1)}, bf16[4,64,256]{2,1,0:T(8,128)(2,1)S(1)}, u32[]{:S(2)}, u32[]{:S(2)}) %collective-permute-start.9) | collective-permute-done | bytes 131104 | tf_op jit(solution)/shard_map/ppermute | solution.py:304
  32.4 6.0 %shard_map.104 = (f32[16,64,256]{2,1,0:T(8,128)S(1)}, bf16[17,64,256]{2,1,0:T(8,128)(2,1)S(1)}) custom-call(bf16[64,16,256]{2,1,0:T(8,128)(2,1)S(1)} %get-tuple-element.26.cube, bf16[16,16,256]{2,1,0:T(8,128)(2,1)S(1)} %collective-permute-done.1.core, bf16[16,16,256]{2,1,0:T(8,128)(2,1)S(1)} %collective-permute-done.2.after.next_, ...), custom_call_target="tpu_custom_call" | custom-call | bytes 1000 | tf_op jit(solution)/shard_map/pallas_call | solution.py:387
  38.5 0.0 collective-permute-done.11.refs_1_
  38.5 0.0 collective-permute-done.12.refs_2_
  38.5 1.0 %collective-permute-done.13.refs_3_ = bf16[4,64,256]{2,1,0:T(8,128)(2,1)S(1)} collective-permute-done((bf16[4,64,256]{2,1,0:T(8,128)(2,1)S(1)}, bf16[4,64,256]{2,1,0:T(8,128)(2,1)S(1)}, u32[]{:S(2)}, u32[]{:S(2)}) %collective-permute-start.13) | collective-permute-done | bytes 131104 | tf_op jit(solution)/shard_map/ppermute | solution.py:304
  39.4 0.0 collective-permute-done.10.refs_0_
  39.4 1.6 %shard_map.105 = (bf16[16,64,256]{2,1,0:T(8,128)(2,1)}, bf16[17,64,256]{2,1,0:T(8,128)(2,1)S(1)}) custom-call(s32[40]{0:T(128)S(1)} %get-tuple-element.25.after.plan, f32[16,64,256]{2,1,0:T(8,128)S(1)} %get-tuple-element.38.hidden, bf16[256,256]{1,0:T(8,128)(2,1)S(1)} %get-tuple-element.39.weight_in, ...), custom_call_target="tpu_custom_call", output_to_operand_aliasing={{1}: (3, {})} | custom-call | bytes 1000 | tf_op jit(solution)/shard_map/pallas_call | solution.py:423
Async XLA Ops:
  0.0 5.0 %collective-permute-start = (bf16[16,64,256]{2,1,0:T(8,128)(2,1)}, bf16[16,64,256]{2,1,0:T(8,128)(2,1)S(1)}, u32[]{:S(2)}, u32[]{:S(2)}) collective-permute-start(bf16[16,64,256]{2,1,0:T(8,128)(2,1)} %previous.1), channel_id=1, source_target_pairs={{0,1},{1,0},{2,3},{3,2},{4,5},{5,4},{6,7},{7,6},{8,9},{9,8},{10,11... | collective-permute-start | bytes 1572872 | tf_op jit(solution)/shard_map/ppermute | solution.py:304
  2.3 8.2 %collective-permute-start.3 = (s32[8]{0:T(128)S(1)}, s32[8]{0:T(128)S(1)}, u32[]{:S(2)}, u32[]{:S(2)}) collective-permute-start(s32[8]{0:T(128)S(1)} %get-tuple-element.30), channel_id=1, source_target_pairs={{0,4},{1,5},{2,6},{3,7},{4,0},{5,1},{6,2},{7,3},{8,12},{9,13},{10,... | collective-permute-start | bytes 104 | tf_op jit(solution)/shard_map/ppermute | solution.py:304
  2.6 8.0 %collective-permute-start.4 = (s32[8]{0:T(128)S(1)}, s32[8]{0:T(128)S(1)}, u32[]{:S(2)}, u32[]{:S(2)}) collective-permute-start(s32[8]{0:T(128)S(1)} %get-tuple-element.31), channel_id=1, source_target_pairs={{0,8},{1,9},{2,10},{3,11},{4,12},{5,13},{6,14},{7,15},{8,0},{9,1},... | collective-permute-start | bytes 104 | tf_op jit(solution)/shard_map/ppermute | solution.py:304
  4.9 5.7 %collective-permute-start.5 = (s32[8]{0:T(128)S(1)}, s32[8]{0:T(128)S(1)}, u32[]{:S(2)}, u32[]{:S(2)}) collective-permute-start(s32[8]{0:T(128)S(1)} %get-tuple-element.32), channel_id=1, source_target_pairs={{0,12},{1,13},{2,14},{3,15},{4,8},{5,9},{6,10},{7,11},{8,4},{9,5},... | collective-permute-start | bytes 104 | tf_op jit(solution)/shard_map/ppermute | solution.py:304
  6.6 14.5 %collective-permute-start.1 = (bf16[16,16,256]{2,1,0:T(8,128)(2,1)S(1)}, bf16[16,16,256]{2,1,0:T(8,128)(2,1)S(1)}, u32[]{:S(2)}, u32[]{:S(2)}) collective-permute-start(bf16[16,16,256]{2,1,0:T(8,128)(2,1)S(1)} %get-tuple-element.27), channel_id=1, source_target_pairs={{0,1},{1,0},{2,3},{3,2},{4,5},{5,4},{6,7},{7,6},{8,9},{9,8},{10,11... | collective-permute-start | bytes 393224 | tf_op jit(solution)/shard_map/ppermute | solution.py:304
  7.5 10.7 %collective-permute-start.2 = (bf16[16,16,256]{2,1,0:T(8,128)(2,1)S(1)}, bf16[16,16,256]{2,1,0:T(8,128)(2,1)S(1)}, u32[]{:S(2)}, u32[]{:S(2)}) collective-permute-start(bf16[16,16,256]{2,1,0:T(8,128)(2,1)S(1)} %get-tuple-element.28), channel_id=1, source_target_pairs={{1,2},{2,1},{3,4},{4,3},{5,6},{6,5},{7,8},{8,7},{9,10},{10,9},{11,... | collective-permute-start | bytes 393224 | tf_op jit(solution)/shard_map/ppermute | solution.py:351
  11.9 10.3 %collective-permute-start.7 = (bf16[4,64,256]{2,1,0:T(8,128)(2,1)S(1)}, bf16[4,64,256]{2,1,0:T(8,128)(2,1)S(1)}, u32[]{:S(2)}, u32[]{:S(2)}) collective-permute-start(bf16[4,64,256]{2,1,0:T(8,128)(2,1)S(1)} %get-tuple-element.35), channel_id=1, source_target_pairs={{0,4},{1,5},{2,6},{3,7},{4,0},{5,1},{6,2},{7,3},{8,12},{9,13},{10,... | collective-permute-start | bytes 393224 | tf_op jit(solution)/shard_map/ppermute | solution.py:304
  13.1 10.5 %collective-permute-start.8 = (bf16[4,64,256]{2,1,0:T(8,128)(2,1)S(1)}, bf16[4,64,256]{2,1,0:T(8,128)(2,1)S(1)}, u32[]{:S(2)}, u32[]{:S(2)}) collective-permute-start(bf16[4,64,256]{2,1,0:T(8,128)(2,1)S(1)} %get-tuple-element.36), channel_id=1, source_target_pairs={{0,8},{1,9},{2,10},{3,11},{4,12},{5,13},{6,14},{7,15},{8,0},{9,1},... | collective-permute-start | bytes 393224 | tf_op jit(solution)/shard_map/ppermute | solution.py:304
  15.3 2.6 %collective-permute-start.6 = (s32[16]{0:T(128)S(1)}, s32[16]{0:T(128)S(1)}, u32[]{:S(2)}, u32[]{:S(2)}) collective-permute-start(s32[16]{0:T(128)S(1)} %get-tuple-element.33), channel_id=1, source_target_pairs={{0,2},{1,3},{2,0},{3,1},{4,6},{5,7},{6,4},{7,5},{8,10},{9,11},{10,... | collective-permute-start | bytes 200 | tf_op jit(solution)/shard_map/ppermute | solution.py:304
  17.9 14.6 %collective-permute-start.9 = (bf16[4,64,256]{2,1,0:T(8,128)(2,1)S(1)}, bf16[4,64,256]{2,1,0:T(8,128)(2,1)S(1)}, u32[]{:S(2)}, u32[]{:S(2)}) collective-permute-start(bf16[4,64,256]{2,1,0:T(8,128)(2,1)S(1)} %get-tuple-element.37), channel_id=1, source_target_pairs={{0,12},{1,13},{2,14},{3,15},{4,8},{5,9},{6,10},{7,11},{8,4},{9,5},... | collective-permute-start | bytes 393224 | tf_op jit(solution)/shard_map/ppermute | solution.py:304
  19.0 19.5 %collective-permute-start.11 = (bf16[4,64,256]{2,1,0:T(8,128)(2,1)S(1)}, bf16[4,64,256]{2,1,0:T(8,128)(2,1)S(1)}, u32[]{:S(2)}, u32[]{:S(2)}) collective-permute-start(bf16[4,64,256]{2,1,0:T(8,128)(2,1)S(1)} %get-tuple-element.41), channel_id=1, source_target_pairs={{0,6},{1,7},{2,4},{3,5},{4,2},{5,3},{6,0},{7,1},{8,14},{9,15},{10,... | collective-permute-start | bytes 393224 | tf_op jit(solution)/shard_map/ppermute | solution.py:304
  21.1 17.4 %collective-permute-start.12 = (bf16[4,64,256]{2,1,0:T(8,128)(2,1)S(1)}, bf16[4,64,256]{2,1,0:T(8,128)(2,1)S(1)}, u32[]{:S(2)}, u32[]{:S(2)}) collective-permute-start(bf16[4,64,256]{2,1,0:T(8,128)(2,1)S(1)} %get-tuple-element.42), channel_id=1, source_target_pairs={{0,10},{1,11},{2,8},{3,9},{4,14},{5,15},{6,12},{7,13},{8,2},{9,3},... | collective-permute-start | bytes 393224 | tf_op jit(solution)/shard_map/ppermute | solution.py:304
  22.3 17.2 %collective-permute-start.13 = (bf16[4,64,256]{2,1,0:T(8,128)(2,1)S(1)}, bf16[4,64,256]{2,1,0:T(8,128)(2,1)S(1)}, u32[]{:S(2)}, u32[]{:S(2)}) collective-permute-start(bf16[4,64,256]{2,1,0:T(8,128)(2,1)S(1)} %get-tuple-element.43), channel_id=1, source_target_pairs={{0,14},{1,15},{2,12},{3,13},{4,10},{5,11},{6,8},{7,9},{8,6},{9,7},... | collective-permute-start | bytes 393224 | tf_op jit(solution)/shard_map/ppermute | solution.py:304
  23.6 15.9 %collective-permute-start.10 = (bf16[4,64,256]{2,1,0:T(8,128)(2,1)S(1)}, bf16[4,64,256]{2,1,0:T(8,128)(2,1)S(1)}, u32[]{:S(2)}, u32[]{:S(2)}) collective-permute-start(bf16[4,64,256]{2,1,0:T(8,128)(2,1)S(1)} %get-tuple-element.34.after), channel_id=1, source_target_pairs={{0,2},{1,3},{2,0},{3,1},{4,6},{5,7},{6,4},{7,5},{8,10},{9,11},{10,... | collective-permute-start | bytes 393224 | tf_op jit(solution)/shard_map/ppermute | solution.py:304
